TPU v7x, 32 devices: a whole 2x2x4 slice. The times are simulated.
32 devices in a mesh: fsdp: 8 (over z, y), fac: 4 (over x, core).
Axes of the slice: x: 2, y: 2, z: 4, core: 2. Of those that a mesh axis runs over, the one named last changes fastest.
Arguments:
- activations: bfloat16 [8192, 3072], P('fsdp'), may hold values from -6 to 6
- out_grads: bfloat16 [8192, 3072], P('fsdp', 'fac'), may hold values from -12 to 12
- token_ids: int32 [8192], P('fsdp'), may hold values from 0 to 32767
- forget_mask: int32 [8192], P('fsdp'), may hold values 0 or 1
- importance: float32 [32768], replicated, may hold values from 0.3 to 3
- in_inverse: bfloat16 [3072, 3072], P('fsdp'), may hold values from -1 to 3, as said below
- out_inverse: bfloat16 [3072, 3072], P(None, 'fac'), may hold values from -1 to 3, as said below
Outputs:
- newton_step: float32 [3072, 3072], P('fsdp', 'fac')
- residual: float32 [3072, 3072], P('fsdp', 'fac')
Inputs may be any that keep to these rules, and one draw needn't show every extreme that they name: `in_inverse`: symmetric and positive definite. `out_inverse`: symmetric and positive definite.
All inputs are finite; a program needn't handle non-finite values. No bound on the sum of `forget_mask` on one device may be relied on, other than what follows from the above.
Results may differ from a plain program's by a relative error of at most 0.03.
Values may be sent and summed in bfloat16 or wider, within the bound.
A program may use at most 64 MiB of HBM per device.

v0:
```python
import math

import jax
import jax.numpy as jnp
from jax import lax
from jax.sharding import PartitionSpec as P

ITERS = 2


damping = 0.3


def add_columns(matrix, piece):
    return jnp.dot(matrix, piece, preferred_element_type=jnp.float32)


def transposed_term(matrix, right):
    return lax.dot_general(
        matrix, right, (((0,), (0,)), ((), ())), preferred_element_type=jnp.float32
    )


def body(activations, out_grads, token_ids, forget_mask, importance, in_inverse, out_inverse):
    tok_rows = activations.shape[0]
    total = tok_rows * lax.axis_size("fsdp")
    keep = 1.0 - forget_mask.astype(jnp.float32)
    weights = importance[token_ids] * keep / total
    forget_grads = out_grads * forget_mask.astype(jnp.bfloat16)[:, None]
    grad_scale = 1.0 / math.sqrt(total)
    gradient = lax.psum_scatter(
        (transposed_term(activations, forget_grads) * grad_scale).astype(jnp.bfloat16),
        "fsdp",
        scatter_dimension=0,
        tiled=True,
    ).astype(jnp.float32)

    def precondition(matrix):
        matrix_low = matrix.astype(jnp.bfloat16)
        mixed = add_columns(in_inverse, lax.all_gather(matrix_low, "fsdp", axis=0, tiled=True))
        mixed_low = mixed.astype(jnp.bfloat16)
        return jnp.dot(
            lax.all_gather(mixed_low, "fac", axis=1, tiled=True),
            out_inverse,
            preferred_element_type=jnp.float32,
        )

    def inner_sum(left, right):
        return lax.psum(jnp.sum(left * right), ("fsdp", "fac"))

    newton_step = jnp.zeros(gradient.shape, jnp.float32)
    residual = -gradient
    precond = precondition(residual)
    direction = precond
    inner_now = inner_sum(residual, precond)
    for iteration in range(ITERS):
        curvature_matrix_low = direction.astype(jnp.bfloat16)
        tok_out = add_columns(
            activations, lax.all_gather(curvature_matrix_low, "fsdp", axis=0, tiled=True)
        )
        scaled = (tok_out * weights[:, None]).astype(jnp.bfloat16)
        local_energy = jnp.sum(tok_out * scaled.astype(jnp.float32)) + damping * jnp.sum(
            direction * direction
        )
        energy = lax.psum(local_energy, ("fsdp", "fac"))
        image = (
            lax.psum_scatter(
                transposed_term(activations, scaled).astype(jnp.bfloat16),
                "fsdp",
                scatter_dimension=0,
                tiled=True,
            ).astype(jnp.float32)
            + damping * direction
        )
        image, energy = (image, energy)
        alpha = inner_now / energy
        newton_step = newton_step + alpha * direction
        residual = residual - alpha * image
        if iteration + 1 < ITERS:
            precond = precondition(residual)
            inner_next = inner_sum(residual, precond)
            direction = precond + inner_next / inner_now * direction
            inner_now = inner_next
    return (newton_step, residual)


def solution(mesh):
    placed = (
        P("fsdp", None),
        P("fsdp", "fac"),
        P("fsdp"),
        P("fsdp"),
        P(),
        P("fsdp", None),
        P(None, "fac"),
    )
    return jax.shard_map(
        body,
        mesh=mesh,
        in_specs=placed,
        out_specs=(P("fsdp", "fac"), P("fsdp", "fac")),
        check_vma=False,
    )
```

profile of v0, /device:TPU:0, one launch (start us, length us, event | category | flops | bytes accessed | tf_op | source)
XLA Modules:
  0.0 811.6 jit_solution(1103198143991578905)
XLA Ops:
  8.1 9.4 %fusion.2 = bf16[3072,768]{0,1:T(8,128)(2,1)} fusion(bf16[1024,3072]{1,0:T(8,128)(2,1)} %param.7, bf16[1024,768]{1,0:T(8,128)(2,1)} %param.8, bf16[1024]{0:T(1024)(128)(2,1)S(1)} %convert_element_type.69), kind=kOutput, calls=%fused_computation.6 | convolution fusion | flops 4837343232 | bytes 12584960 | tf_op jit(solution)/shard_map/dot_general | solution.py:19
  17.5 6.6 copy.28
  24.2 98.1 %reduce-scatter.10.cloned.1.call-done = bf16[384,768]{1,0:T(8,128)(2,1)} async-done(((bf16[3072,768]{1,0:T(8,128)(2,1)}), bf16[384,768]{1,0:T(8,128)(2,1)}) %reduce-scatter.10.cloned.1.call-update) | async-done | bytes 589840 | tf_op jit(solution)/shard_map/reduce_scatter | solution.py:31
  124.3 80.4 %all-gather.7.cloned.1.call-done = bf16[3072,768]{1,0:T(8,128)(2,1)} async-done(((bf16[384,768]{1,0:T(8,128)(2,1)}), bf16[3072,768]{1,0:T(8,128)(2,1)}) %all-gather.7.cloned.1.call-update) | async-done | bytes 4718608 | tf_op jit(solution)/shard_map/all_gather | solution.py:40
  210.5 22.3 %all-gather.9.cloned.1.call-done = bf16[384,3072]{0,1:T(8,128)(2,1)} async-done(((bf16[384,768]{0,1:T(8,128)(2,1)}), bf16[384,3072]{0,1:T(8,128)(2,1)}) %all-gather.9.cloned.1.call-update) | async-done | bytes 2359312 | tf_op jit(solution)/shard_map/all_gather | solution.py:43
  232.8 7.0 multiply_reduce_fusion.2
  240.8 6.1 gather_fusion
  246.9 73.0 %all-gather.11.cloned.1.call-done = bf16[3072,768]{1,0:T(8,128)(2,1)} async-done(((bf16[384,768]{1,0:T(8,128)(2,1)}), bf16[3072,768]{1,0:T(8,128)(2,1)}) %all-gather.11.cloned.1.call-update) | async-done | bytes 4718608 | tf_op jit(solution)/shard_map/all_gather | solution.py:59
  319.9 9.6 %fusion.6 = (f32[]{:T(128)}, f32[768,1024]{1,0:T(8,128)S(1)}) fusion(f32[1024]{0:T(1024)S(1)} %multiply_multiply_fusion, bf16[3072,768]{1,0:T(8,128)(2,1)} %all-gather.11.cloned.1.call-done, bf16[1024,3072]{1,0:T(8,128)(2,1)} %param.7), kind=kOutput, calls=%fused_computation.14 | convolution fusion | flops 4835770368 | bytes 14159876 | tf_op jit(solution)/shard_map/dot_general | solution.py:15
  329.5 9.5 %fusion = bf16[3072,768]{0,1:T(8,128)(2,1)} fusion(bf16[1024,3072]{1,0:T(8,128)(2,1)} %param.7, f32[768,1024]{1,0:T(8,128)S(1)} %get-tuple-element.19, f32[1024]{0:T(1024)S(1)} %multiply_multiply_fusion), kind=kOutput, calls=%fused_computation.4 | convolution fusion | flops 4835770368 | bytes 14159872 | tf_op jit(solution)/shard_map/dot_general | solution.py:19
  339.0 6.6 copy.30
  347.1 41.1 %all-reduce = (f32[]{:T(128)}, f32[]{:T(128)}) all-reduce(f32[]{:T(128)} %get-tuple-element.7, f32[]{:T(128)S(6)} %add.40), channel_id=1, replica_groups=mesh['fsdp'=8,'fac'=4] {'fsdp','fac'}, use_global_device_ids=true, to_apply=%region_2.0 | all-reduce | flops 2 | bytes 16 | tf_op jit(solution)/shard_map/psum | solution.py:49
  389.5 50.8 %reduce-scatter.12.cloned.1.call-done = bf16[384,768]{1,0:T(8,128)(2,1)} async-done(((bf16[3072,768]{1,0:T(8,128)(2,1)}), bf16[384,768]{1,0:T(8,128)(2,1)}) %reduce-scatter.12.cloned.1.call-update) | async-done | bytes 589840 | tf_op jit(solution)/shard_map/reduce_scatter | solution.py:67
  443.1 79.7 %all-gather.13.cloned.1.call-done = bf16[3072,768]{1,0:T(8,128)(2,1)} async-done(((bf16[384,768]{1,0:T(8,128)(2,1)}), bf16[3072,768]{1,0:T(8,128)(2,1)}) %all-gather.13.cloned.1.call-update) | async-done | bytes 4718608 | tf_op jit(solution)/shard_map/all_gather | solution.py:40
  522.8 5.8 fusion.11
  528.7 22.3 %all-gather.15.cloned.1.call-done = bf16[384,3072]{0,1:T(8,128)(2,1)} async-done(((bf16[384,768]{0,1:T(8,128)(2,1)}), bf16[384,3072]{0,1:T(8,128)(2,1)}) %all-gather.15.cloned.1.call-update) | async-done | bytes 2359312 | tf_op jit(solution)/shard_map/all_gather | solution.py:43
  551.0 6.1 multiply_reduce_fusion.1
  557.1 39.5 %psum.30 = f32[]{:T(128)} all-reduce(f32[]{:T(128)} %get-tuple-element.20), channel_id=1, replica_groups=mesh['fsdp'=8,'fac'=4] {'fsdp','fac'}, use_global_device_ids=true, to_apply=%region_8.0 | all-reduce | flops 1 | bytes 8 | tf_op jit(solution)/shard_map/psum | solution.py:49
  600.2 80.8 %all-gather.17.cloned.1.call-done = bf16[3072,768]{1,0:T(8,128)(2,1)} async-done(((bf16[384,768]{1,0:T(8,128)(2,1)}), bf16[3072,768]{1,0:T(8,128)(2,1)}) %all-gather.17.cloned.1.call-update) | async-done | bytes 4718608 | tf_op jit(solution)/shard_map/all_gather | solution.py:59
  681.0 9.6 %fusion.4 = (f32[]{:T(128)}, f32[768,1024]{1,0:T(8,128)S(1)}) fusion(f32[1024]{0:T(1024)S(1)} %multiply_multiply_fusion, bf16[3072,768]{1,0:T(8,128)(2,1)} %all-gather.17.cloned.1.call-done, bf16[1024,3072]{1,0:T(8,128)(2,1)} %param.7), kind=kOutput, calls=%fused_computation.10 | convolution fusion | flops 4835770368 | bytes 14159876 | tf_op jit(solution)/shard_map/dot_general | solution.py:15
  690.6 9.5 %fusion.1 = bf16[3072,768]{0,1:T(8,128)(2,1)} fusion(bf16[1024,3072]{1,0:T(8,128)(2,1)} %param.7, f32[768,1024]{1,0:T(8,128)S(1)} %get-tuple-element.23, f32[1024]{0:T(1024)S(1)} %multiply_multiply_fusion), kind=kOutput, calls=%fused_computation.5 | convolution fusion | flops 4835770368 | bytes 14159872 | tf_op jit(solution)/shard_map/dot_general | solution.py:19
  700.1 6.6 copy.32
  708.0 40.5 %psum.31 = f32[]{:T(128)} all-reduce(f32[]{:T(128)S(6)} %add.43), channel_id=1, replica_groups=mesh['fsdp'=8,'fac'=4] {'fsdp','fac'}, use_global_device_ids=true, to_apply=%region_11.0 | all-reduce | flops 1 | bytes 8 | tf_op jit(solution)/shard_map/psum | solution.py:65
  750.1 51.5 %reduce-scatter.14.cloned.1.call-done = bf16[384,768]{1,0:T(8,128)(2,1)} async-done(((bf16[3072,768]{1,0:T(8,128)(2,1)}), bf16[384,768]{1,0:T(8,128)(2,1)}) %reduce-scatter.14.cloned.1.call-update) | async-done | bytes 589840 | tf_op jit(solution)/shard_map/reduce_scatter | solution.py:67
  (43 shorter events, 18.4 us)
Async XLA Ops:
  7.2 197.5 %copy-start = (bf16[384,3072]{1,0:T(8,128)(2,1)S(1)}, bf16[384,3072]{1,0:T(8,128)(2,1)}, u32[]{:S(2)}) copy-start(bf16[384,3072]{1,0:T(8,128)(2,1)} %param.12) | copy-start | bytes 7077892
  7.2 115.0 %reduce-scatter.10.cloned.1.call-start = ((), (), s32[]{:S(2)}) async-start(), calls=%async_computation.9 | async-start | bytes 5308416 | tf_op jit(solution)/shard_map/reduce_scatter | solution.py:31
  24.1 180.5 %all-gather.7.cloned.1.call-start = ((), (), s32[]{:S(2)}) async-start(), calls=%async_computation.3 | async-start | bytes 5308416 | tf_op jit(solution)/shard_map/all_gather | solution.py:40
  124.2 108.6 %copy-start.5 = (bf16[384,768]{1,0:T(8,128)(2,1)S(1)}, bf16[384,768]{1,0:T(8,128)(2,1)}, u32[]{:S(2)}) copy-start(bf16[384,768]{1,0:T(8,128)(2,1)} %reduce-scatter.10.cloned.1.call-done) | copy-start | bytes 1769476
  124.2 108.6 %all-gather.9.cloned.1.call-start = ((), (), s32[]{:S(2)}) async-start(), calls=%async_computation.4 | async-start | bytes 2949120 | tf_op jit(solution)/shard_map/all_gather | solution.py:43
  210.5 29.6 %copy-start.7 = (s32[1024]{0:T(1024)S(1)}, s32[1024]{0:T(1024)}, u32[]{:S(2)}) copy-start(s32[1024]{0:T(1024)} %param.9) | copy-start | bytes 12292
  210.5 109.4 %all-gather.11.cloned.1.call-start = ((), (), s32[]{:S(2)}) async-start(), calls=%async_computation.5 | async-start | bytes 5308416 | tf_op jit(solution)/shard_map/all_gather | solution.py:59
  239.8 0.9 copy-start.2
  239.9 7.1 copy-start.6
  239.9 200.4 %reduce-scatter.12.cloned.1.call-start = ((), (), s32[]{:S(2)}) async-start(), calls=%async_computation.10 | async-start | bytes 5308416 | tf_op jit(solution)/shard_map/reduce_scatter | solution.py:67
  345.6 94.6 %copy-start.3 = (f32[384,768]{1,0:T(8,128)S(1)}, f32[384,768]{1,0:T(8,128)}, u32[]{:S(2)}) copy-start(f32[384,768]{1,0:T(8,128)} %get-tuple-element.17) | copy-start | bytes 3538948
  345.7 177.2 %all-gather.13.cloned.1.call-start = ((), (), s32[]{:S(2)}) async-start(), calls=%async_computation.6 | async-start | bytes 5308416 | tf_op jit(solution)/shard_map/all_gather | solution.py:40
  443.0 108.0 %all-gather.15.cloned.1.call-start = ((), (), s32[]{:S(2)}) async-start(), calls=%async_computation.7 | async-start | bytes 2949120 | tf_op jit(solution)/shard_map/all_gather | solution.py:43
  528.6 152.4 %all-gather.17.cloned.1.call-start = ((), (), s32[]{:S(2)}) async-start(), calls=%async_computation.8 | async-start | bytes 5308416 | tf_op jit(solution)/shard_map/all_gather | solution.py:59
  599.0 91.6 %copy-start.4 = (f32[384,768]{1,0:T(8,128)}, f32[384,768]{1,0:T(8,128)S(1)}, u32[]{:S(2)}) copy-start(f32[384,768]{1,0:T(8,128)S(1)} %get-tuple-element.11) | copy-start | bytes 3538948
  600.0 201.6 %reduce-scatter.14.cloned.1.call-start = ((), (), s32[]{:S(2)}) async-start(), calls=%async_computation.11 | async-start | bytes 5308416 | tf_op jit(solution)/shard_map/reduce_scatter | solution.py:67
  748.5 56.5 %copy-start.1 = (bf16[384,3072]{1,0:T(8,128)(2,1)S(1)}, bf16[384,3072]{1,0:T(8,128)(2,1)}, u32[]{:S(2)}) copy-start(bf16[384,3072]{1,0:T(8,128)(2,1)} %param.12) | copy-start | bytes 7077892
Sparse Core Ops, SparseCore 0:
  24.2 97.9 reduce-scatter.9
  125.0 79.6 all-gather.6
  210.6 22.1 all-gather.8
  240.0 79.8 all-gather.10
  345.8 94.4 reduce-scatter.11
  443.1 79.6 all-gather.12
  528.8 22.1 all-gather.14
  600.1 80.8 all-gather.16
  706.9 94.6 reduce-scatter.13
where the time goes:
time: 813 us; the launch traced here: 812 us
  waiting for transfers between devices  559 us (69%)
  blocking collectives  121 us (15%)
  matrix products  72.3 us (9%)
  local copies, waits for them, and re-layouts  26.7 us (3%)
  between operations  20.8 us (3%)
  other arithmetic  11 us (1%)
    all_gather x2, waiting for transfers between devices, precondition(): lax.all_gather(matrix_low, 'fsdp', axis=0, tiled=True)  160 us
    all_gather x2, waiting for transfers between devices, body(): lax.all_gather(curvature_matrix_low, 'fsdp', axis=0, tiled=True)  154 us
    reduce_scatter x2, waiting for transfers between devices, body(): lax.psum_scatter(transposed_term(activations, scaled).astype(jnp.bfloat16...  102 us
    reduce_scatter x1, waiting for transfers between devices, body(): lax.psum_scatter((transposed_term(activations, forget_grads) * grad_scale...  98.1 us
    psum x2, blocking collectives, inner_sum(): return lax.psum(jnp.sum(left * right), ('fsdp', 'fac'))  80.6 us
    all_gather x2, waiting for transfers between devices, precondition(): lax.all_gather(mixed_low, 'fac', axis=1, tiled=True)  44.6 us
    psum x1, blocking collectives, body(): energy = lax.psum(local_energy, ('fsdp', 'fac'))  40.5 us
    dot_general x4, matrix products, add_columns(): return jnp.dot(matrix, piece, preferred_element_type=jnp.float32)  30.7 us
  transfers between devices with their start and end apart: 9, of which 9 were waited for; matrix products, arithmetic and copies ran while one was open for 1% of the time, Pallas kernels for 0%

commit v1 on v0

v1 whole, which is shorter than its diff:
```python
import math

import jax
import jax.numpy as jnp
from jax import lax
from jax.sharding import PartitionSpec as P

damping = 0.3


def product(left, right):
    return jnp.dot(left, right, preferred_element_type=jnp.float32)


def transposed_term(matrix, right):
    return lax.dot_general(
        matrix, right, (((0,), (0,)), ((), ())), preferred_element_type=jnp.float32
    )


def body(activations, out_grads, token_ids, forget_mask, importance, in_inverse, out_inverse):
    low = jnp.bfloat16
    tok_rows = activations.shape[0]
    total = tok_rows * lax.axis_size("fsdp")
    columns = out_inverse.shape[1]
    own = lax.axis_index("fac") * columns

    def rows_sum(partial):
        return lax.psum_scatter(partial, "fsdp", scatter_dimension=0, tiled=True)

    def all_rows(block):
        return lax.all_gather(block, "fsdp", axis=0, tiled=True)

    def all_columns(block):
        return lax.all_gather(block, "fac", axis=1, tiled=True)

    in_block = lax.dynamic_slice(in_inverse, (0, own), (in_inverse.shape[0], columns))
    in_columns = all_rows(in_block)

    keep = 1.0 - forget_mask.astype(jnp.float32)
    weights = importance[token_ids] * keep / total
    forget_grads = out_grads * forget_mask.astype(low)[:, None]
    grad_scale = 1.0 / math.sqrt(total)
    gradient_low = rows_sum((transposed_term(activations, forget_grads) * grad_scale).astype(low))

    tok_out = product(activations, in_columns)
    scaled = (tok_out * weights[:, None]).astype(low)
    both_block = rows_sum(transposed_term(activations, scaled).astype(low)).astype(jnp.float32)
    both_block = (both_block + damping * in_block.astype(jnp.float32)).astype(low)
    both = all_columns(both_block)

    def mix(matrix_low):
        return all_rows(product(all_columns(matrix_low), out_inverse).astype(low))

    start_low = -gradient_low
    start = start_low.astype(jnp.float32)
    mixed = mix(start_low)
    image_0 = product(both, mixed)
    precond_0 = product(in_inverse, mixed)
    mixed = mix(image_0.astype(low))
    precond_1 = product(in_inverse, mixed)
    image_1 = product(both, mixed)

    pairs = (
        (start, precond_0),
        (precond_0, image_0),
        (start, precond_1),
        (image_0, precond_1),
        (precond_0, image_1),
        (precond_1, image_1),
    )
    sums = lax.psum(jnp.stack([jnp.sum(a * b) for a, b in pairs]), ("fsdp", "fac"))
    return finish(start, precond_0, image_0, precond_1, image_1, sums)


def finish(start, precond_0, image_0, precond_1, image_1, sums):
    rz, energy, rq, wq, zv, qv = [sums[i] for i in range(6)]
    alpha = rz / energy
    rz_new = rz - alpha * (energy + rq) + alpha * alpha * wq
    grow = 1.0 + rz_new / rz
    energy_new = grow * grow * energy - grow * alpha * (zv + wq) + alpha * alpha * qv
    alpha_new = rz_new / energy_new
    first = alpha + alpha_new * grow
    second = alpha * alpha_new
    newton_step = first * precond_0 - second * precond_1
    residual = start - first * image_0 + second * image_1
    return newton_step, residual


def solution(mesh):
    placed = (
        P("fsdp", None),
        P("fsdp", "fac"),
        P("fsdp"),
        P("fsdp"),
        P(),
        P("fsdp", None),
        P(None, "fac"),
    )
    return jax.shard_map(
        body,
        mesh=mesh,
        in_specs=placed,
        out_specs=(P("fsdp", "fac"), P("fsdp", "fac")),
        check_vma=False,
    )
```

time: 813 us -> 615 us (0.76)
  waiting for transfers between devices: 559 us -> 448 us
  blocking collectives: 121 us -> 38.4 us
  matrix products: 72.3 us -> 61 us
  local copies, waits for them, and re-layouts: 26.7 us -> 37.9 us
    reduce_scatter x3 -> x0, waiting for transfers between devices: 200 us -> none  [the longest x2 102 us: body(): lax.psum_scatter(transposed_term(activations, scaled).astype(jnp.bfloat16...]
    unnamed x9 -> x10, waiting for transfers between devices: 0.15 us -> 169 us
    psum x3 -> x1, blocking collectives: 121 us -> 38.4 us  [body(): lax.psum(jnp.stack([jnp.sum(a * b) for a, b in pairs]), ('fsdp', 'fac'))]
    all_gather x6, waiting for transfers between devices: 359 us -> 278 us  [the longest x3 215 us: all_rows(): return lax.all_gather(block, 'fsdp', axis=0, tiled=True)]
    dot_general x6, matrix products: 43.8 us -> 34.1 us  [product(): return jnp.dot(left, right, preferred_element_type=jnp.float32)]
    unnamed x19 -> x27, local copies, waits for them, and re-layouts: 20.6 us -> 24.6 us
    dot_general x3 -> x2, matrix products: 28.4 us -> 26.9 us  [transposed_term(): lax.dot_general(matrix, right, (((0,), (0,)), ((), ())), preferred_elemen...]
  transfers between devices with their start and end apart: 9 -> 8, of which waited for: 9 -> 8; matrix products, arithmetic and copies ran while one was open for 1% -> 11% of each run, Pallas kernels for 0% -> 0%
where the time goes in v1:
time: 615 us; the launch traced here: 614 us
  waiting for transfers between devices  448 us (73%)
  matrix products  61 us (10%)
  blocking collectives  38.4 us (6%)
  local copies, waits for them, and re-layouts  37.9 us (6%)
  between operations  21.2 us (3%)
  other arithmetic  7.11 us (1%)
    all_gather x3, waiting for transfers between devices, all_rows(): return lax.all_gather(block, 'fsdp', axis=0, tiled=True)  215 us
    unnamed x10, waiting for transfers between devices  169 us
    all_gather x3, waiting for transfers between devices, all_columns(): return lax.all_gather(block, 'fac', axis=1, tiled=True)  63.3 us
    psum x1, blocking collectives, body(): lax.psum(jnp.stack([jnp.sum(a * b) for a, b in pairs]), ('fsdp', 'fac'))  38.4 us
    dot_general x6, matrix products, product(): return jnp.dot(left, right, preferred_element_type=jnp.float32)  34.1 us
    dot_general x2, matrix products, transposed_term(): lax.dot_general(matrix, right, (((0,), (0,)), ((), ())), preferred_elemen...  26.9 us
    unnamed x27, local copies, waits for them, and re-layouts  24.6 us
  transfers between devices with their start and end apart: 8, of which 8 were waited for; matrix products, arithmetic and copies ran while one was open for 11% of the time, Pallas kernels for 0%

profile of v1, /device:TPU:0, one launch (start us, length us, event | category | flops | bytes accessed | tf_op | source)
XLA Modules:
  0.0 613.7 jit_solution(6311336237208252333)
XLA Ops:
  10.0 9.3 %fusion.1 = bf16[3072,768]{0,1:T(8,128)(2,1)} fusion(bf16[1024,3072]{1,0:T(8,128)(2,1)} %param.7, bf16[1024,768]{1,0:T(8,128)(2,1)} %param.8, bf16[1024]{0:T(1024)(128)(2,1)S(1)} %convert_element_type.43), kind=kOutput, calls=%fused_computation.4 | convolution fusion | flops 4837343232 | bytes 12584960 | tf_op jit(solution)/shard_map/dot_general | solution.py:16
  19.4 6.7 %copy.37 = bf16[3072,768]{1,0:T(8,128)(2,1)} copy(bf16[3072,768]{0,1:T(8,128)(2,1)} %fusion.1) | data formatting | bytes 9437184
  27.0 6.1 %gather_fusion = f32[1024]{0:T(1024)S(1)} fusion(f32[32768]{0:T(1024)S(1)} %copy-done.1, s32[1024]{0:T(1024)S(1)} %fusion.7), kind=kCustom, calls=%fused_computation | custom fusion | bytes 12288 | tf_op jit(solution)/shard_map/gather | solution.py:41
  33.2 61.2 %all-gather.11.cloned.1.call-done = bf16[3072,768]{0,1:T(8,128)(2,1)} async-done(((bf16[384,768]{0,1:T(8,128)(2,1)}), bf16[3072,768]{0,1:T(8,128)(2,1)}) %all-gather.11.cloned.1.call-update) | async-done | bytes 4718608 | tf_op jit(solution)/shard_map/all_gather | solution.py:32
  94.4 17.6 %fusion = bf16[3072,768]{0,1:T(8,128)(2,1)} fusion(bf16[1024,3072]{1,0:T(8,128)(2,1)} %param.7, bf16[3072,768]{0,1:T(8,128)(2,1)} %all-gather.11.cloned.1.call-done, f32[1024]{0:T(1024)S(1)} %multiply_multiply_fusion), kind=kOutput, calls=%fused_computation.3 | convolution fusion | flops 9667608576 | bytes 15732736 | tf_op jit(solution)/shard_map/dot_general | solution.py:16
  112.0 6.8 %copy.39 = bf16[3072,768]{1,0:T(8,128)(2,1)} copy(bf16[3072,768]{0,1:T(8,128)(2,1)} %fusion) | data formatting | bytes 9437184
  118.8 72.7 %reduce-scatter.7.cloned.1.call-done = bf16[384,768]{1,0:T(8,128)(2,1)} async-done(((bf16[3072,768]{1,0:T(8,128)(2,1)}), bf16[384,768]{1,0:T(8,128)(2,1)}) %reduce-scatter.7.cloned.1.call-update) | async-done | bytes 589840
  193.9 96.4 %reduce-scatter.9.cloned.1.call-done = bf16[384,768]{1,0:T(8,128)(2,1)} async-done(((bf16[3072,768]{1,0:T(8,128)(2,1)}), bf16[384,768]{1,0:T(8,128)(2,1)}) %reduce-scatter.9.cloned.1.call-update) | async-done | bytes 589840
  294.6 21.0 %all-gather.7.cloned.1.call-done = bf16[384,3072]{0,1:T(8,128)(2,1)} async-done(((bf16[384,768]{0,1:T(8,128)(2,1)}), bf16[384,3072]{0,1:T(8,128)(2,1)}) %all-gather.7.cloned.1.call-update) | async-done | bytes 2359312 | tf_op jit(solution)/shard_map/all_gather | solution.py:35
  315.6 5.9 convolution_convert_fusion.2
  321.7 19.9 %all-gather.13.cloned.1.call-done = bf16[384,3072]{0,1:T(8,128)(2,1)} async-done(((bf16[384,768]{0,1:T(8,128)(2,1)}), bf16[384,3072]{0,1:T(8,128)(2,1)}) %all-gather.13.cloned.1.call-update) | async-done | bytes 2359312 | tf_op jit(solution)/shard_map/all_gather | solution.py:35
  341.7 82.5 %all-gather.9.cloned.1.call-done = bf16[3072,768]{1,0:T(8,128)(2,1)} async-done(((bf16[384,768]{1,0:T(8,128)(2,1)}), bf16[3072,768]{1,0:T(8,128)(2,1)}) %all-gather.9.cloned.1.call-update) | async-done | bytes 4718608 | tf_op jit(solution)/shard_map/all_gather | solution.py:32
  424.2 6.3 %fusion.9 = (bf16[384,768]{1,0:T(8,128)(2,1)}, f32[384,768]{1,0:T(8,128)}) fusion(bf16[384,3072]{0,1:T(8,128)(2,1)} %all-gather.13.cloned.1.call-done, bf16[3072,768]{1,0:T(8,128)(2,1)} %all-gather.9.cloned.1.call-done), kind=kOutput, calls=%fused_computation.29 | convolution fusion | flops 1812234240 | bytes 8847360 | tf_op jit(solution)/shard_map/dot_general | solution.py:12
  430.6 22.3 %all-gather.15.cloned.1.call-done = bf16[384,3072]{1,0:T(8,128)(2,1)} async-done(((bf16[384,768]{1,0:T(8,128)(2,1)}), bf16[384,3072]{1,0:T(8,128)(2,1)}) %all-gather.15.cloned.1.call-update) | async-done | bytes 2359312 | tf_op jit(solution)/shard_map/all_gather | solution.py:35
  452.9 5.9 convolution_convert_fusion.1
  458.8 2.7 copy.28
  461.5 6.0 convolution_bitcast_fusion.1
  467.5 71.3 %all-gather.17.cloned.1.call-done = bf16[3072,768]{1,0:T(8,128)(2,1)} async-done(((bf16[384,768]{1,0:T(8,128)(2,1)}), bf16[3072,768]{1,0:T(8,128)(2,1)}) %all-gather.17.cloned.1.call-update) | async-done | bytes 4718608 | tf_op jit(solution)/shard_map/all_gather | solution.py:32
  538.9 5.4 fusion.10
  544.3 4.5 multiply_reduce_fusion
  548.9 3.8 stack.27
  552.7 38.4 %psum.7 = f32[6]{0:T(128)S(1)} all-reduce(f32[6]{0:T(128)S(1)} %stack.27), channel_id=1, replica_groups=mesh['fsdp'=8,'fac'=4] {'fsdp','fac'}, use_global_device_ids=true, to_apply=%region_8.0 | all-reduce | flops 6 | bytes 48 | tf_op jit(solution)/shard_map/psum | solution.py:72
  598.7 4.1 fusion.5
  602.7 2.7 copy.35
  (47 shorter events, 12.8 us)
Async XLA Ops:
  7.2 1.7 copy-start
  7.2 2.8 copy-start.7
  7.2 87.2 %all-gather.11.cloned.1.call-start = ((), (), s32[]{:S(2)}) async-start(), calls=%async_computation.4 | async-start | bytes 5308416 | tf_op jit(solution)/shard_map/all_gather | solution.py:32
  10.0 181.5 %reduce-scatter.7.cloned.1.call-start = ((), (), s32[]{:S(2)}) async-start(), calls=%async_computation.8 | async-start | bytes 5308416
  26.1 0.7 copy-start.8
  26.1 0.9 copy-start.1
  26.1 264.2 %reduce-scatter.9.cloned.1.call-start = ((), (), s32[]{:S(2)}) async-start(), calls=%async_computation.9 | async-start | bytes 5308416
  118.8 173.7 %copy-start.2 = (bf16[384,768]{0,1:T(8,128)(2,1)S(1)}, bf16[384,768]{0,1:T(8,128)(2,1)}, u32[]{:S(2)}) copy-start(bf16[384,768]{0,1:T(8,128)(2,1)} %copy.41) | copy-start | bytes 1769476
  118.8 196.8 %all-gather.7.cloned.1.call-start = ((), (), s32[]{:S(2)}) async-start(), calls=%async_computation.2 | async-start | bytes 2949120 | tf_op jit(solution)/shard_map/all_gather | solution.py:35
  193.9 147.8 %all-gather.13.cloned.1.call-start = ((), (), s32[]{:S(2)}) async-start(), calls=%async_computation.5 | async-start | bytes 2949120 | tf_op jit(solution)/shard_map/all_gather | solution.py:35
  294.5 129.7 %all-gather.9.cloned.1.call-start = ((), (), s32[]{:S(2)}) async-start(), calls=%async_computation.3 | async-start | bytes 5308416 | tf_op jit(solution)/shard_map/all_gather | solution.py:32
  321.5 131.4 %all-gather.15.cloned.1.call-start = ((), (), s32[]{:S(2)}) async-start(), calls=%async_computation.6 | async-start | bytes 2949120 | tf_op jit(solution)/shard_map/all_gather | solution.py:35
  430.5 108.3 %all-gather.17.cloned.1.call-start = ((), (), s32[]{:S(2)}) async-start(), calls=%async_computation.7 | async-start | bytes 5308416 | tf_op jit(solution)/shard_map/all_gather | solution.py:32
  538.8 5.4 copy-start.3
  538.8 5.4 copy-start.5
  538.8 5.5 copy-start.9
  544.3 4.5 copy-start.6
  602.7 2.8 copy-start.4
Sparse Core Ops, SparseCore 0:
  10.7 83.6 all-gather.10
  98.0 93.4 reduce-scatter.6
  195.2 95.1 reduce-scatter.8
  291.7 23.7 all-gather.6
  317.6 24.0 all-gather.12
  344.3 79.8 all-gather.8
  430.6 22.1 all-gather.14
  458.9 79.8 all-gather.16

commit v2 on v1

--- a/solution.py
+++ b/solution.py
@@ -1,11 +1,16 @@
+import functools
 import math
 
 import jax
 import jax.numpy as jnp
 from jax import lax
+from jax.experimental import pallas as pl
+from jax.experimental.pallas import tpu as pltpu
 from jax.sharding import PartitionSpec as P
 
 damping = 0.3
+MESH = pl.DeviceIdType.MESH
+VMEM_BYTES = 40 * 1024 * 1024
 
 
 def product(left, right):
@@ -16,6 +21,247 @@
     return lax.dot_general(
         matrix, right, (((0,), (0,)), ((), ())), preferred_element_type=jnp.float32
     )
+
+
+def index_at(place, n):
+    odd = place // (n // 2)
+    return 2 * (place + odd * (n - 1 - 2 * place)) + odd
+
+
+def ring(n):
+    me = lax.axis_index("fsdp")
+    pair = me // 2
+    place = pair + (me % 2) * (n - 1 - 2 * pair)
+    return me, place, index_at((place + 1) % n, n), index_at((place + n - 1) % n, n)
+
+
+def greet(neighbours):
+    barrier = pltpu.get_barrier_semaphore()
+    for neighbour in neighbours:
+        pl.semaphore_signal(barrier, inc=1, device_id=neighbour, device_id_type=MESH)
+    pl.semaphore_wait(barrier, len(neighbours))
+
+
+def gather_kernel(n, lefts, *refs):
+    left_refs, block_ref = refs[:lefts], refs[lefts]
+    full_ref, product_refs = refs[lefts + 1], refs[lefts + 2 : 2 * lefts + 2]
+    send_sem, recv_sem = refs[2 * lefts + 2 :]
+    rows, columns = block_ref.shape
+    half, piece = columns // 2, rows // 2
+    me, place, following, preceding = ring(n)
+    greet(({"fsdp": following}, {"fsdp": preceding}))
+
+    full_ref[pl.ds(pl.multiple_of(me * rows, rows), rows), :] = block_ref[...]
+
+    def owner_at(step, way):
+        return index_at((place + n - step) % n if way == 0 else (place + step) % n, n)
+
+    def copy(step, way, part):
+        at = full_ref.at[
+            pl.ds(pl.multiple_of(owner_at(step, way) * rows + part * piece, piece), piece),
+            pl.ds(way * half, half),
+        ]
+        return pltpu.make_async_remote_copy(
+            src_ref=at,
+            dst_ref=at,
+            send_sem=send_sem.at[step, way, part],
+            recv_sem=recv_sem.at[step, way, part],
+            device_id={"fsdp": following if way == 0 else preceding},
+            device_id_type=MESH,
+        )
+
+    for way in range(2):
+        for part in range(2):
+            copy(0, way, part).start()
+    for ref in product_refs:
+        ref[...] = jnp.zeros_like(ref)
+
+    def step_body(step, carry):
+        for way in range(2):
+            for part in range(2):
+
+                @pl.when(step > 0)
+                def _():
+                    copy(step - 1, way, part).wait_recv()
+
+                @pl.when((step > 0) & (step < n - 1))
+                def _():
+                    copy(step, way, part).start()
+
+        for way in range(2):
+            at = pl.ds(pl.multiple_of(owner_at(step, way) * rows, rows), rows)
+            block = full_ref[at, way * half : (way + 1) * half]
+            for left_ref, ref in zip(left_refs, product_refs):
+                ref[:, way * half : (way + 1) * half] += product(left_ref[:, at], block)
+        return carry
+
+    lax.fori_loop(0, n, step_body, 0)
+
+    def settle(step, carry):
+        for way in range(2):
+            for part in range(2):
+                copy(step, way, part).wait_send()
+        return carry
+
+    lax.fori_loop(0, n - 1, settle, 0)
+
+
+def gather_products(lefts, block, number):
+    n = lax.axis_size("fsdp")
+    rows, columns = block.shape
+    vmem = pl.BlockSpec(memory_space=pltpu.VMEM)
+    outs = [jax.ShapeDtypeStruct((n * rows, columns), block.dtype)]
+    outs += [jax.ShapeDtypeStruct((left.shape[0], columns), jnp.float32) for left in lefts]
+    return pl.pallas_call(
+        functools.partial(gather_kernel, n, len(lefts)),
+        out_shape=outs,
+        in_specs=[vmem] * (len(lefts) + 1),
+        out_specs=[vmem] * len(outs),
+        scratch_shapes=[pltpu.SemaphoreType.DMA((n - 1, 2, 2))] * 2,
+        compiler_params=pltpu.CompilerParams(
+            collective_id=number, has_side_effects=True, vmem_limit_bytes=VMEM_BYTES
+        ),
+        cost_estimate=pl.CostEstimate(
+            flops=2 * n * rows * columns * sum(left.shape[0] for left in lefts),
+            bytes_accessed=2 * n * rows * columns * 8,
+            transcendentals=0,
+        ),
+    )(*lefts, block)
+
+
+def scatter_kernel(n, factor, left_ref, right_ref, out_ref, own, sent, held, send_sem, recv_sem):
+    rows, columns = out_ref.shape
+    half, piece = columns // 2, rows // 2
+    me, place, following, preceding = ring(n)
+    greet(({"fsdp": following}, {"fsdp": preceding}))
+
+    def copy(step, way, part):
+        return pltpu.make_async_remote_copy(
+            src_ref=sent.at[step, way, part],
+            dst_ref=held.at[step, way, part],
+            send_sem=send_sem.at[step, way, part],
+            recv_sem=recv_sem.at[step, way, part],
+            device_id={"fsdp": following if way == 0 else preceding},
+            device_id_type=MESH,
+        )
+
+    def step_body(step, carry):
+        for way in range(2):
+            target = index_at((place + 2 * n - 1 - step) % n if way == 0 else (place + 1 + step) % n, n)
+            at = pl.ds(pl.multiple_of(target * rows, rows), rows)
+            own[way] = transposed_term(left_ref[:, at], right_ref[:, way * half : (way + 1) * half])
+        for part in range(2):
+            for way in range(2):
+                lines = slice(part * piece, (part + 1) * piece)
+
+                @pl.when(step == 0)
+                def _():
+                    sent[step, way, part] = (own[way, lines, :] * factor).astype(sent.dtype)
+
+                @pl.when(step > 0)
+                def _():
+                    copy(step - 1, way, part).wait_recv()
+                    term = held[step - 1, way, part].astype(jnp.float32)
+                    term = term + own[way, lines, :] * factor
+
+                    @pl.when(step < n - 1)
+                    def _():
+                        sent[step, way, part] = term.astype(sent.dtype)
+
+                    @pl.when(step == n - 1)
+                    def _():
+                        out_ref[lines, way * half : (way + 1) * half] = term
+
+                @pl.when(step < n - 1)
+                def _():
+                    copy(step, way, part).start()
+
+        return carry
+
+    lax.fori_loop(0, n, step_body, 0)
+
+    def settle(step, carry):
+        for way in range(2):
+            for part in range(2):
+                copy(step, way, part).wait_send()
+        return carry
+
+    lax.fori_loop(0, n - 1, settle, 0)
+
+
+def scatter_term(left, right, factor, number):
+    n = lax.axis_size("fsdp")
+    rows, columns = left.shape[1] // n, right.shape[1]
+    vmem = pl.BlockSpec(memory_space=pltpu.VMEM)
+    slots = pltpu.VMEM((n - 1, 2, 2, rows // 2, columns // 2), jnp.bfloat16)
+    return pl.pallas_call(
+        functools.partial(scatter_kernel, n, factor),
+        out_shape=jax.ShapeDtypeStruct((rows, columns), jnp.float32),
+        in_specs=[vmem] * 2,
+        out_specs=vmem,
+        scratch_shapes=[
+            pltpu.VMEM((2, rows, columns // 2), jnp.float32),
+            slots,
+            slots,
+            pltpu.SemaphoreType.DMA((n - 1, 2, 2)),
+            pltpu.SemaphoreType.DMA((n - 1, 2, 2)),
+        ],
+        compiler_params=pltpu.CompilerParams(
+            collective_id=number, has_side_effects=True, vmem_limit_bytes=VMEM_BYTES
+        ),
+        cost_estimate=pl.CostEstimate(
+            flops=2 * left.shape[0] * left.shape[1] * columns,
+            bytes_accessed=2 * n * rows * columns * 8,
+            transcendentals=0,
+        ),
+    )(left, right)
+
+
+def sum_kernel(sizes, own_ref, out_ref, sent, held, send_sem, recv_sem):
+    stages = []
+    for axis, size in sizes:
+        me = lax.axis_index(axis)
+        bit = 1
+        while bit < size:
+            stages.append({axis: me + bit * (1 - 2 * ((me // bit) % 2))})
+            bit *= 2
+    greet(stages)
+    total = own_ref[...]
+    for number, partner in enumerate(stages):
+        sent[number] = total
+        copy = pltpu.make_async_remote_copy(
+            src_ref=sent.at[number],
+            dst_ref=held.at[number],
+            send_sem=send_sem.at[number],
+            recv_sem=recv_sem.at[number],
+            device_id=partner,
+            device_id_type=MESH,
+        )
+        copy.start()
+        copy.wait()
+        total = total + held[number]
+    out_ref[...] = total
+
+
+def sum_everywhere(values, number):
+    sizes = [(axis, lax.axis_size(axis)) for axis in ("fac", "fsdp")]
+    if any(size & (size - 1) for _, size in sizes):
+        return lax.psum(values, ("fsdp", "fac"))
+    stages = sum(size.bit_length() - 1 for _, size in sizes)
+    vmem = pl.BlockSpec(memory_space=pltpu.VMEM)
+    return pl.pallas_call(
+        functools.partial(sum_kernel, sizes),
+        out_shape=jax.ShapeDtypeStruct(values.shape, values.dtype),
+        in_specs=[vmem],
+        out_specs=vmem,
+        scratch_shapes=[
+            pltpu.VMEM((stages, *values.shape), values.dtype),
+            pltpu.VMEM((stages, *values.shape), values.dtype),
+            pltpu.SemaphoreType.DMA((stages,)),
+            pltpu.SemaphoreType.DMA((stages,)),
+        ],
+        compiler_params=pltpu.CompilerParams(collective_id=number, has_side_effects=True),
+    )(values)
 
 
 def body(activations, out_grads, token_ids, forget_mask, importance, in_inverse, out_inverse):
@@ -25,8 +271,16 @@
     columns = out_inverse.shape[1]
     own = lax.axis_index("fac") * columns
 
-    def rows_sum(partial):
-        return lax.psum_scatter(partial, "fsdp", scatter_dimension=0, tiled=True)
+    shards = lax.axis_size("fsdp")
+    rows = in_inverse.shape[0]
+    ringed = shards % 2 == 0 and rows % 128 == 0 and columns % 256 == 0
+
+    def rows_sum(right, factor, number):
+        if ringed:
+            return scatter_term(activations, right, factor, number)
+        partial = (transposed_term(activations, right) * factor).astype(low)
+        partial = lax.psum_scatter(partial, "fsdp", scatter_dimension=0, tiled=True)
+        return partial.astype(jnp.float32)
 
     def all_rows(block):
         return lax.all_gather(block, "fsdp", axis=0, tiled=True)
@@ -41,25 +295,31 @@
     weights = importance[token_ids] * keep / total
     forget_grads = out_grads * forget_mask.astype(low)[:, None]
     grad_scale = 1.0 / math.sqrt(total)
-    gradient_low = rows_sum((transposed_term(activations, forget_grads) * grad_scale).astype(low))
+    start = -rows_sum(forget_grads, grad_scale, 0)
 
     tok_out = product(activations, in_columns)
     scaled = (tok_out * weights[:, None]).astype(low)
-    both_block = rows_sum(transposed_term(activations, scaled).astype(low)).astype(jnp.float32)
+    both_block = rows_sum(scaled, 1.0, 1)
     both_block = (both_block + damping * in_block.astype(jnp.float32)).astype(low)
     both = all_columns(both_block)
 
-    def mix(matrix_low):
-        return all_rows(product(all_columns(matrix_low), out_inverse).astype(low))
-
-    start_low = -gradient_low
-    start = start_low.astype(jnp.float32)
-    mixed = mix(start_low)
+    def mix(matrix):
+        return product(all_columns(matrix.astype(low)), out_inverse).astype(low)
+
+    mixed = mix(start)
+    if ringed:
+        mixed, precond_0 = gather_products((in_inverse,), mixed, 2)
+    else:
+        mixed = all_rows(mixed)
+        precond_0 = product(in_inverse, mixed)
     image_0 = product(both, mixed)
-    precond_0 = product(in_inverse, mixed)
-    mixed = mix(image_0.astype(low))
-    precond_1 = product(in_inverse, mixed)
-    image_1 = product(both, mixed)
+    mixed = mix(image_0)
+    if ringed:
+        _, precond_1, image_1 = gather_products((in_inverse, both), mixed, 3)
+    else:
+        mixed = all_rows(mixed)
+        precond_1 = product(in_inverse, mixed)
+        image_1 = product(both, mixed)
 
     pairs = (
         (start, precond_0),
@@ -69,7 +329,11 @@
         (precond_0, image_1),
         (precond_1, image_1),
     )
-    sums = lax.psum(jnp.stack([jnp.sum(a * b) for a, b in pairs]), ("fsdp", "fac"))
+    lane = lax.broadcasted_iota(jnp.int32, (8, 128), 1)
+    local = jnp.zeros((8, 128), jnp.float32)
+    for number, (left, right) in enumerate(pairs):
+        local = jnp.where(lane == number, jnp.sum(left * right), local)
+    sums = sum_everywhere(local, 4)[0]
     return finish(start, precond_0, image_0, precond_1, image_1, sums)
 
 

time: 615 us -> 368 us (0.60)
  waiting for transfers between devices: 448 us -> 29.2 us
  Pallas kernels: 0 us -> 261 us
  blocking collectives: 38.4 us -> 0 us
  matrix products: 61 us -> 25.1 us
  local copies, waits for them, and re-layouts: 37.9 us -> 18.1 us
    pallas_call x0 -> x5, Pallas kernels: none -> 261 us  [the longest x2 145 us: scatter_term(): pl.pallas_call(functools.partial(scatter_kernel, n, factor), out_shape=ja...]
    all_gather x3 -> x1, waiting for transfers between devices: 215 us -> 5.78 us  [all_rows(): return lax.all_gather(block, 'fsdp', axis=0, tiled=True)]
    unnamed x10 -> x4, waiting for transfers between devices: 169 us -> 0.07 us
    all_gather x3, waiting for transfers between devices: 63.3 us -> 23.3 us  [all_columns(): return lax.all_gather(block, 'fac', axis=1, tiled=True)]
    psum x1 -> x0, blocking collectives: 38.4 us -> none  [body(): lax.psum(jnp.stack([jnp.sum(a * b) for a, b in pairs]), ('fsdp', 'fac'))]
    dot_general x2 -> x0, matrix products: 26.9 us -> none  [transposed_term(): lax.dot_general(matrix, right, (((0,), (0,)), ((), ())), preferred_elemen...]
    unnamed x27 -> x26, local copies, waits for them, and re-layouts: 24.6 us -> 8.36 us
    dot_general x6 -> x4, matrix products: 34.1 us -> 25.1 us  [product(): return jnp.dot(left, right, preferred_element_type=jnp.float32)]
  transfers between devices with their start and end apart: 8 -> 4, of which waited for: 8 -> 2; matrix products, arithmetic and copies ran while one was open for 11% -> 6% of each run, Pallas kernels for 0% -> 53%
where the time goes in v2:
time: 368 us; the launch traced here: 367 us
  Pallas kernels  261 us (71%)
  waiting for transfers between devices  29.2 us (8%)
  matrix products  25.1 us (7%)
  between operations  21.1 us (6%)
  local copies, waits for them, and re-layouts  18.1 us (5%)
  other arithmetic  12.7 us (3%)
    pallas_call x2, Pallas kernels, scatter_term(): pl.pallas_call(functools.partial(scatter_kernel, n, factor), out_shape=ja...  145 us
    pallas_call x2, Pallas kernels, gather_products(): pl.pallas_call(functools.partial(gather_kernel, n, len(lefts)), out_shape...  100 us
    dot_general x4, matrix products, product(): return jnp.dot(left, right, preferred_element_type=jnp.float32)  25.1 us
    all_gather x3, waiting for transfers between devices, all_columns(): return lax.all_gather(block, 'fac', axis=1, tiled=True)  23.3 us
    pallas_call x1, Pallas kernels, sum_everywhere(): pl.pallas_call(functools.partial(sum_kernel, sizes), out_shape=jax.ShapeD...  15 us
    unnamed x26, local copies, waits for them, and re-layouts  8.36 us
  transfers between devices with their start and end apart: 4, of which 2 were waited for; matrix products, arithmetic and copies ran while one was open for 6% of the time, Pallas kernels for 53%

profile of v2, /device:TPU:0, one launch (start us, length us, event | category | flops | bytes accessed | tf_op | source)
XLA Modules:
  0.0 367.3 jit_solution(1463967738482349770)
XLA Ops:
  7.2 2.0 constant_dynamic-slice_fusion
  9.6 2.8 copy-done.5
  12.4 94.8 %shard_map.87 = f32[384,768]{1,0:T(8,128)S(1)} custom-call(bf16[1024,3072]{1,0:T(8,128)(2,1)S(1)} %copy-done.5, bf16[1024,768]{1,0:T(8,128)(2,1)S(1)} %broadcast_multiply_fusion.right_ref), custom_call_target="tpu_custom_call" | custom-call | flops 4831838208 | bytes 37748736 | tf_op jit(solution)/shard_map/pallas_call | solution.py:197
  107.2 0.9 negate_convert_fusion
  108.2 6.2 %gather_fusion = f32[1024]{0:T(1024)S(1)} fusion(f32[32768]{0:T(1024)S(1)} %copy-done, s32[1024]{0:T(1024)S(1)} %fusion.1), kind=kCustom, calls=%fused_computation | custom fusion | bytes 12288 | tf_op jit(solution)/shard_map/gather | solution.py:295
  114.4 5.8 %all-gather.5.cloned.1.call-done = bf16[3072,768]{1,0:T(8,128)(2,1)} async-done(((bf16[384,768]{1,0:T(8,128)(2,1)}), bf16[3072,768]{1,0:T(8,128)(2,1)}) %all-gather.5.cloned.1.call-update) | async-done | bytes 4718608 | tf_op jit(solution)/shard_map/all_gather | solution.py:286
  120.2 8.5 %fusion.right_ref = bf16[1024,768]{1,0:T(8,128)(2,1)S(1)} fusion(f32[1024]{0:T(1024)S(1)} %multiply_multiply_fusion, bf16[1024,3072]{1,0:T(8,128)(2,1)} %left_ref.3, bf16[3072,768]{1,0:T(8,128)(2,1)} %all-gather.5.cloned.1.call-done), kind=kOutput, calls=%fused_computation.2 | convolution fusion | flops 4833411072 | bytes 12587008 | tf_op jit(solution)/shard_map/dot_general | solution.py:17
  128.7 3.4 copy-done.6
  132.1 50.5 %shard_map.86 = f32[384,768]{1,0:T(8,128)S(1)} custom-call(bf16[1024,3072]{1,0:T(8,128)(2,1)S(1)} %copy-done.6, bf16[1024,768]{1,0:T(8,128)(2,1)S(1)} %fusion.right_ref), custom_call_target="tpu_custom_call" | custom-call | flops 4831838208 | bytes 37748736 | tf_op jit(solution)/shard_map/pallas_call | solution.py:197
  182.6 2.0 add_convert_fusion
  184.7 0.2 all-gather.11.cloned.1.call-start
  184.9 5.2 %convolution_convert_fusion.1.refs_1_ = bf16[384,768]{1,0:T(8,128)(2,1)S(1)} fusion(bf16[384,3072]{1,0:T(8,128)(2,1)} %all-gather.9.cloned.1.call-done, bf16[3072,768]{1,0:T(8,128)(2,1)} %param.13), kind=kOutput, calls=%fused_computation.4 | convolution fusion | flops 1812234240 | bytes 7667712 | tf_op jit(solution)/shard_map/dot_general | solution.py:17
  190.1 47.9 %shard_map.88 = (bf16[3072,768]{1,0:T(8,128)(2,1)S(1)}, f32[384,768]{1,0:T(8,128)S(1)}) custom-call(bf16[384,3072]{1,0:T(8,128)(2,1)S(1)} %copy-done.3, bf16[384,768]{1,0:T(8,128)(2,1)S(1)} %convolution_convert_fusion.1.refs_1_), custom_call_target="tpu_custom_call" | custom-call | flops 1811939328 | bytes 37748736 | tf_op jit(solution)/shard_map/pallas_call | solution.py:115
  238.1 2.1 copy-done.8
  240.2 6.2 %fusion.3 = (bf16[384,768]{1,0:T(8,128)(2,1)}, f32[384,768]{1,0:T(8,128)}) fusion(bf16[384,3072]{1,0:T(8,128)(2,1)} %all-gather.7.cloned.1.call-done.refs_1_, bf16[3072,768]{1,0:T(8,128)(2,1)} %copy-done.8), kind=kOutput, calls=%fused_computation.28 | convolution fusion | flops 1812234240 | bytes 8847360 | tf_op jit(solution)/shard_map/dot_general | solution.py:17
  246.6 23.3 %all-gather.11.cloned.1.call-done = bf16[384,3072]{1,0:T(8,128)(2,1)} async-done(((bf16[384,768]{1,0:T(8,128)(2,1)}), bf16[384,3072]{1,0:T(8,128)(2,1)}) %all-gather.11.cloned.1.call-update) | async-done | bytes 2359312 | tf_op jit(solution)/shard_map/all_gather | solution.py:289
  269.9 5.2 %convolution_convert_fusion.refs_2_ = bf16[384,768]{1,0:T(8,128)(2,1)S(1)} fusion(bf16[384,3072]{1,0:T(8,128)(2,1)} %all-gather.11.cloned.1.call-done, bf16[3072,768]{1,0:T(8,128)(2,1)} %param.13), kind=kOutput, calls=%fused_computation.3 | convolution fusion | flops 1812234240 | bytes 7667712 | tf_op jit(solution)/shard_map/dot_general | solution.py:17
  275.1 52.5 %shard_map.89 = (bf16[3072,768]{1,0:T(8,128)(2,1)}, f32[384,768]{1,0:T(8,128)S(1)}, f32[384,768]{1,0:T(8,128)S(1)}) custom-call(bf16[384,3072]{1,0:T(8,128)(2,1)S(1)} %copy-done.4, bf16[384,3072]{1,0:T(8,128)(2,1)S(1)} %copy-done.7, bf16[384,768]{1,0:T(8,128)(2,1)S(1)} %convolution_convert_fusion.refs_2_), custom_call_target="tpu_custom_call" | custom-call | flops 3623878656 | bytes 37748736 | tf_op jit(solution)/shard_map/pallas_call | solution.py:115
  327.6 1.5 multiply_reduce_fusion.5
  329.1 0.7 compare_select_fusion.1
  329.8 3.6 select_select_fusion.own_ref
  333.4 15.0 %shard_map.90 = f32[8,128]{1,0:T(8,128)} custom-call(f32[8,128]{1,0:T(8,128)} %select_select_fusion.own_ref), custom_call_target="tpu_custom_call" | custom-call | tf_op jit(solution)/shard_map/pallas_call | solution.py:252
  348.4 1.6 fusion.2
  357.0 3.8 %multiply_add_fusion = (f32[384,768]{1,0:T(8,128)}, f32[384,768]{1,0:T(8,128)}) fusion(f32[384,768]{1,0:T(8,128)} %copy-done.2, f32[384,768]{1,0:T(8,128)} %get-tuple-element.23, f32[384,768]{1,0:T(8,128)S(1)} %shard_map.87, f32[]{:T(128)S(6)} %mul.123, f32[]{:T(128)S(6)} %add.42, f32[384,768]{1,0:T(8,128)} %copy-done.1, f32[384,768]{1,0:T(8,128)S(1)} %get-tuple-element.9), kind=kLoop, calls=%fused_computation.5 | loop fusion | flops 2359296 | bytes 8257544 | tf_op jit(solution)/shard_map/add | solution.py:350
  (41 shorter events, 0.5 us)
Async XLA Ops:
  7.2 101.0 %copy-start = (f32[32768]{0:T(1024)S(1)}, f32[32768]{0:T(1024)}, u32[]{:S(2)}) copy-start(f32[32768]{0:T(1024)} %param.11) | copy-start | bytes 393220
  7.2 2.2 copy-start.11
  7.2 2.2 copy-start.10
  7.2 113.0 %all-gather.5.cloned.1.call-start = ((), (), s32[]{:S(2)}) async-start(), calls=%async_computation | async-start | bytes 5308416 | tf_op jit(solution)/shard_map/all_gather | solution.py:286
  9.3 175.6 %all-gather.9.cloned.1.call-start = ((), (), s32[]{:S(2)}) async-start(), calls=%async_computation.2 | async-start | bytes 2949120 | tf_op jit(solution)/shard_map/all_gather | solution.py:289
  9.6 2.8 copy-start.5
  107.2 1.0 copy-start.12
  108.1 132.1 %all-gather.7.cloned.1.call-start = ((), (), s32[]{:S(2)}) async-start(), calls=%async_computation.1 | async-start | bytes 2949120 | tf_op jit(solution)/shard_map/all_gather | solution.py:289
  128.7 3.4 copy-start.6
  184.7 85.2 %all-gather.11.cloned.1.call-start = ((), (), s32[]{:S(2)}) async-start(), calls=%async_computation.3 | async-start | bytes 2949120 | tf_op jit(solution)/shard_map/all_gather | solution.py:289
  184.9 5.2 %copy-start.3 = (bf16[384,3072]{1,0:T(8,128)(2,1)S(1)}, bf16[384,3072]{1,0:T(8,128)(2,1)}, u32[]{:S(2)}) copy-start(bf16[384,3072]{1,0:T(8,128)(2,1)} %refs_0_.3) | copy-start | bytes 7077892
  238.1 2.1 copy-start.8
  269.9 5.2 %copy-start.4 = (bf16[384,3072]{1,0:T(8,128)(2,1)S(1)}, bf16[384,3072]{1,0:T(8,128)(2,1)}, u32[]{:S(2)}) copy-start(bf16[384,3072]{1,0:T(8,128)(2,1)} %refs_0_.3) | copy-start | bytes 7077892
  269.9 5.2 %copy-start.7 = (bf16[384,3072]{1,0:T(8,128)(2,1)S(1)}, bf16[384,3072]{1,0:T(8,128)(2,1)}, u32[]{:S(2)}) copy-start(bf16[384,3072]{1,0:T(8,128)(2,1)} %all-gather.7.cloned.1.call-done.refs_1_) | copy-start | bytes 7077892
  275.1 52.6 %copy-start.9 = (f32[384,768]{1,0:T(8,128)S(1)}, f32[384,768]{1,0:T(8,128)}, u32[]{:S(2)}) copy-start(f32[384,768]{1,0:T(8,128)} %get-tuple-element.23) | copy-start | bytes 3538948
  327.6 1.5 copy-start.1
  327.6 1.5 copy-start.2
Sparse Core Ops, SparseCore 0:
  10.8 109.3 all-gather.4
  122.3 24.6 all-gather.8
  184.8 23.1 all-gather.6
  246.6 23.1 all-gather.10

commit v3 on v2

--- a/solution.py
+++ b/solution.py
@@ -217,51 +217,170 @@
     )(left, right)
 
 
-def sum_kernel(sizes, own_ref, out_ref, sent, held, send_sem, recv_sem):
+def spread_kernel(both_ref, mixed_ref, right_ref, image_ref, out_ref, held, send_sem, recv_sem):
+    rows, columns = image_ref.shape
+    piece = rows // 2
+    me = lax.axis_index("fac")
+    beside = {"fac": me + 1 - 2 * (me % 2)}
+    across = {"fac": (me + 2) % 4}
+    greet((beside, across))
+
+    def copy(number, part):
+        source, slot, to = ((0, 1, beside), (0, 2, across), (2, 3, beside))[number]
+        return pltpu.make_async_remote_copy(
+            src_ref=held.at[source, part],
+            dst_ref=held.at[slot, part],
+            send_sem=send_sem.at[number, part],
+            recv_sem=recv_sem.at[number, part],
+            device_id=to,
+            device_id_type=MESH,
+        )
+
+    def add(slot, owner):
+        at = pl.ds(pl.multiple_of(owner * columns, columns), columns)
+        for part in range(2):
+            term = product(held[slot, part], right_ref[at, :])
+            lines = slice(part * piece, (part + 1) * piece)
+            image = term if slot == 0 else term + total[part]
+            total[part] = image
+            if slot == 3:
+                out_ref[lines, :] = image.astype(out_ref.dtype)
+
+    total = [None, None]
+    for part in range(2):
+        lines = slice(part * piece, (part + 1) * piece)
+        image_ref[lines, :] = product(both_ref[lines, :], mixed_ref[...])
+        held[0, part] = image_ref[lines, :].astype(held.dtype)
+        copy(1, part).start()
+        copy(0, part).start()
+    add(0, me)
+    for part in range(2):
+        copy(0, part).wait_recv()
+    add(1, me + 1 - 2 * (me % 2))
+    for part in range(2):
+        copy(1, part).wait_recv()
+        copy(2, part).start()
+    add(2, (me + 2) % 4)
+    for part in range(2):
+        copy(2, part).wait_recv()
+    add(3, (me + 1 - 2 * (me % 2) + 2) % 4)
+    for number in range(3):
+        for part in range(2):
+            copy(number, part).wait_send()
+
+
+def spread(both, mixed, right, number):
+    rows, columns = both.shape[0], mixed.shape[1]
+    vmem = pl.BlockSpec(memory_space=pltpu.VMEM)
+    return pl.pallas_call(
+        spread_kernel,
+        out_shape=(
+            jax.ShapeDtypeStruct((rows, columns), jnp.float32),
+            jax.ShapeDtypeStruct((rows, columns), jnp.bfloat16),
+        ),
+        in_specs=[vmem] * 3,
+        out_specs=(vmem, vmem),
+        scratch_shapes=[
+            pltpu.VMEM((4, 2, rows // 2, columns), jnp.bfloat16),
+            pltpu.SemaphoreType.DMA((3, 2)),
+            pltpu.SemaphoreType.DMA((3, 2)),
+        ],
+        compiler_params=pltpu.CompilerParams(
+            collective_id=number, has_side_effects=True, vmem_limit_bytes=VMEM_BYTES
+        ),
+        cost_estimate=pl.CostEstimate(
+            flops=2 * rows * columns * (both.shape[1] + right.shape[0]),
+            bytes_accessed=2 * (mixed.size + right.size),
+            transcendentals=0,
+        ),
+    )(both, mixed, right)
+
+
+PAIRS = ((0, 1), (1, 2), (0, 3), (2, 3), (1, 4), (3, 4))
+
+
+def finish_kernel(sizes, *refs):
+    blocks, outs = refs[:5], refs[5:7]
+    sent, held, send_sem, recv_sem = refs[7:]
+    rows, columns = outs[0].shape
+
     stages = []
     for axis, size in sizes:
         me = lax.axis_index(axis)
-        bit = 1
-        while bit < size:
-            stages.append({axis: me + bit * (1 - 2 * ((me // bit) % 2))})
-            bit *= 2
-    greet(stages)
-    total = own_ref[...]
-    for number, partner in enumerate(stages):
-        sent[number] = total
-        copy = pltpu.make_async_remote_copy(
-            src_ref=sent.at[number],
-            dst_ref=held.at[number],
-            send_sem=send_sem.at[number],
-            recv_sem=recv_sem.at[number],
-            device_id=partner,
-            device_id_type=MESH,
-        )
-        copy.start()
-        copy.wait()
-        total = total + held[number]
-    out_ref[...] = total
-
-
-def sum_everywhere(values, number):
+        stages.append([{axis: (me + away) % size} for away in range(1, size)])
+    greet(stages[0] + stages[1])
+
+    def lines_at(row):
+        return pl.ds(pl.multiple_of(row * 8, 8), 8)
+
+    def add_row(row, sums):
+        values = [ref[lines_at(row), :] for ref in blocks]
+        return tuple(total + values[a] * values[b] for total, (a, b) in zip(sums, PAIRS))
+
+    sums = lax.fori_loop(0, rows // 8, add_row, (jnp.zeros((8, columns), jnp.float32),) * len(PAIRS))
+    sums = [sum(one[:, lane : lane + 128] for lane in range(0, columns, 128)) for one in sums]
+    slot = 0
+    for stage, peers in enumerate(stages):
+        for number, one in enumerate(sums):
+            sent[stage, number] = one
+        copies = []
+        for peer in peers:
+            copies.append(
+                pltpu.make_async_remote_copy(
+                    src_ref=sent.at[stage],
+                    dst_ref=held.at[slot],
+                    send_sem=send_sem.at[slot],
+                    recv_sem=recv_sem.at[slot],
+                    device_id=peer,
+                    device_id_type=MESH,
+                )
+            )
+            copies[-1].start()
+            slot += 1
+        for place, one in enumerate(copies):
+            one.wait()
+            at = slot - len(copies) + place
+            sums = [total + held[at, number] for number, total in enumerate(sums)]
+
+    rz, energy, rq, wq, zv, qv = [jnp.sum(one, axis=(0, 1), keepdims=True) for one in sums]
+    alpha = rz / energy
+    rz_new = rz - alpha * (energy + rq) + alpha * alpha * wq
+    grow = 1.0 + rz_new / rz
+    energy_new = grow * grow * energy - grow * alpha * (zv + wq) + alpha * alpha * qv
+    alpha_new = rz_new / energy_new
+    first = jnp.broadcast_to(alpha + alpha_new * grow, (8, columns))
+    second = jnp.broadcast_to(alpha * alpha_new, (8, columns))
+
+    def write_row(row, carry):
+        at = lines_at(row)
+        start, precond_0, image_0, precond_1, image_1 = [ref[at, :] for ref in blocks]
+        outs[0][at, :] = first * precond_0 - second * precond_1
+        outs[1][at, :] = start - first * image_0 + second * image_1
+        return carry
+
+    lax.fori_loop(0, rows // 8, write_row, 0)
+
+
+def finish(blocks, number):
     sizes = [(axis, lax.axis_size(axis)) for axis in ("fac", "fsdp")]
-    if any(size & (size - 1) for _, size in sizes):
-        return lax.psum(values, ("fsdp", "fac"))
-    stages = sum(size.bit_length() - 1 for _, size in sizes)
+    peers = sum(size - 1 for _, size in sizes)
     vmem = pl.BlockSpec(memory_space=pltpu.VMEM)
+    shape = jax.ShapeDtypeStruct(blocks[0].shape, jnp.float32)
     return pl.pallas_call(
-        functools.partial(sum_kernel, sizes),
-        out_shape=jax.ShapeDtypeStruct(values.shape, values.dtype),
-        in_specs=[vmem],
-        out_specs=vmem,
+        functools.partial(finish_kernel, sizes),
+        out_shape=(shape, shape),
+        in_specs=[vmem] * 5,
+        out_specs=(vmem, vmem),
         scratch_shapes=[
-            pltpu.VMEM((stages, *values.shape), values.dtype),
-            pltpu.VMEM((stages, *values.shape), values.dtype),
-            pltpu.SemaphoreType.DMA((stages,)),
-            pltpu.SemaphoreType.DMA((stages,)),
+            pltpu.VMEM((2, len(PAIRS), 8, 128), jnp.float32),
+            pltpu.VMEM((peers, len(PAIRS), 8, 128), jnp.float32),
+            pltpu.SemaphoreType.DMA((peers,)),
+            pltpu.SemaphoreType.DMA((peers,)),
         ],
-        compiler_params=pltpu.CompilerParams(collective_id=number, has_side_effects=True),
-    )(values)
+        compiler_params=pltpu.CompilerParams(
+            collective_id=number, has_side_effects=True, vmem_limit_bytes=VMEM_BYTES
+        ),
+    )(*blocks)
 
 
 def body(activations, out_grads, token_ids, forget_mask, importance, in_inverse, out_inverse):
@@ -289,17 +408,20 @@
         return lax.all_gather(block, "fac", axis=1, tiled=True)
 
     in_block = lax.dynamic_slice(in_inverse, (0, own), (in_inverse.shape[0], columns))
-    in_columns = all_rows(in_block)
+    if ringed:
+        _, tok_out = gather_products((activations,), in_block, 0)
+    else:
+        tok_out = product(activations, all_rows(in_block))
 
     keep = 1.0 - forget_mask.astype(jnp.float32)
     weights = importance[token_ids] * keep / total
     forget_grads = out_grads * forget_mask.astype(low)[:, None]
     grad_scale = 1.0 / math.sqrt(total)
-    start = -rows_sum(forget_grads, grad_scale, 0)
-
-    tok_out = product(activations, in_columns)
     scaled = (tok_out * weights[:, None]).astype(low)
-    both_block = rows_sum(scaled, 1.0, 1)
+    forget_grads, scaled = lax.optimization_barrier((forget_grads, scaled))
+    start = -rows_sum(forget_grads, grad_scale, 1)
+    start, scaled = lax.optimization_barrier((start, scaled))
+    both_block = rows_sum(scaled, 1.0, 2)
     both_block = (both_block + damping * in_block.astype(jnp.float32)).astype(low)
     both = all_columns(both_block)
 
@@ -308,47 +430,23 @@
 
     mixed = mix(start)
     if ringed:
-        mixed, precond_0 = gather_products((in_inverse,), mixed, 2)
+        mixed, precond_0 = gather_products((in_inverse,), mixed, 3)
     else:
         mixed = all_rows(mixed)
         precond_0 = product(in_inverse, mixed)
-    image_0 = product(both, mixed)
-    mixed = mix(image_0)
+    if ringed and lax.axis_size("fac") == 4:
+        image_0, mixed = spread(both, mixed, out_inverse, 4)
+    else:
+        image_0 = product(both, mixed)
+        mixed = mix(image_0)
     if ringed:
-        _, precond_1, image_1 = gather_products((in_inverse, both), mixed, 3)
+        _, precond_1, image_1 = gather_products((in_inverse, both), mixed, 5)
     else:
         mixed = all_rows(mixed)
         precond_1 = product(in_inverse, mixed)
         image_1 = product(both, mixed)
 
-    pairs = (
-        (start, precond_0),
-        (precond_0, image_0),
-        (start, precond_1),
-        (image_0, precond_1),
-        (precond_0, image_1),
-        (precond_1, image_1),
-    )
-    lane = lax.broadcasted_iota(jnp.int32, (8, 128), 1)
-    local = jnp.zeros((8, 128), jnp.float32)
-    for number, (left, right) in enumerate(pairs):
-        local = jnp.where(lane == number, jnp.sum(left * right), local)
-    sums = sum_everywhere(local, 4)[0]
-    return finish(start, precond_0, image_0, precond_1, image_1, sums)
-
-
-def finish(start, precond_0, image_0, precond_1, image_1, sums):
-    rz, energy, rq, wq, zv, qv = [sums[i] for i in range(6)]
-    alpha = rz / energy
-    rz_new = rz - alpha * (energy + rq) + alpha * alpha * wq
-    grow = 1.0 + rz_new / rz
-    energy_new = grow * grow * energy - grow * alpha * (zv + wq) + alpha * alpha * qv
-    alpha_new = rz_new / energy_new
-    first = alpha + alpha_new * grow
-    second = alpha * alpha_new
-    newton_step = first * precond_0 - second * precond_1
-    residual = start - first * image_0 + second * image_1
-    return newton_step, residual
+    return finish((start, precond_0, image_0, precond_1, image_1), 6)
 
 
 def solution(mesh):

time: 368 us -> 328 us (0.89)
  waiting for transfers between devices: 29.2 us -> 0.06 us
  Pallas kernels: 261 us -> 282 us
  matrix products: 25.1 us -> 5.19 us
  other arithmetic: 12.7 us -> 4.81 us
  between operations: 21.1 us -> 14.3 us
    pallas_call x2 -> x3, Pallas kernels: 100 us -> 156 us  [gather_products(): pl.pallas_call(functools.partial(gather_kernel, n, len(lefts)), out_shape...]
    pallas_call x2, Pallas kernels: 145 us -> 95.8 us  [scatter_term(): pl.pallas_call(functools.partial(scatter_kernel, n, factor), out_shape=ja...]
    all_gather x3 -> x2, waiting for transfers between devices: 23.3 us -> 0.02 us  [all_columns(): return lax.all_gather(block, 'fac', axis=1, tiled=True)]
    dot_general x4 -> x1, matrix products: 25.1 us -> 5.19 us  [product(): return jnp.dot(left, right, preferred_element_type=jnp.float32)]
    pallas_call x1 -> x2, Pallas kernels: 15 us -> 30.3 us  [the longest x1 18.4 us: spread(): pl.pallas_call(spread_kernel, out_shape=(jax.ShapeDtypeStruct((rows, colu...]
    all_gather x1 -> x0, waiting for transfers between devices: 5.78 us -> none  [all_rows(): return lax.all_gather(block, 'fsdp', axis=0, tiled=True)]
    unnamed x26 -> x28, local copies, waits for them, and re-layouts: 8.36 us -> 13.3 us
    select_n x2 -> x0, other arithmetic: 4.32 us -> none  [body(): local = jnp.where(lane == number, jnp.sum(left * right), local)]
  transfers between devices with their start and end apart: 4 -> 2, of which waited for: 2 -> 0; matrix products, arithmetic and copies ran while one was open for 6% -> 2% of each run, Pallas kernels for 53% -> 29%
where the time goes in v3:
time: 328 us
  Pallas kernels  282 us (86%)
  local copies, waits for them, and re-layouts  20.6 us (6%)
  between operations  14.3 us (4%)
  matrix products  5.19 us (2%)
  other arithmetic  4.81 us (1%)
    pallas_call x3, Pallas kernels, gather_products(): pl.pallas_call(functools.partial(gather_kernel, n, len(lefts)), out_shape...  156 us
    pallas_call x2, Pallas kernels, scatter_term(): pl.pallas_call(functools.partial(scatter_kernel, n, factor), out_shape=ja...  95.8 us
    pallas_call x1, Pallas kernels, spread(): pl.pallas_call(spread_kernel, out_shape=(jax.ShapeDtypeStruct((rows, colu...  18.4 us
    unnamed x28, local copies, waits for them, and re-layouts  13.3 us
    pallas_call x1, Pallas kernels, finish(): pl.pallas_call(functools.partial(finish_kernel, sizes), out_shape=(shape,...  11.9 us
  transfers between devices with their start and end apart: 2, of which 0 were waited for; matrix products, arithmetic and copies ran while one was open for 2% of the time, Pallas kernels for 29%

profile of v3, /device:TPU:0, one launch (start us, length us, event | category | flops | bytes accessed | tf_op | source)
XLA Modules:
  0.0 327.6 jit_solution(18094986171598461871)
XLA Ops:
  7.2 0.7 convert_element_type.21
  7.9 0.7 fusion
  8.6 6.2 %gather_fusion = f32[1024]{0:T(1024)S(1)} fusion(f32[32768]{0:T(1024)S(1)} %copy-done, s32[1024]{0:T(1024)S(1)} %fusion), kind=kCustom, calls=%fused_computation | custom fusion | bytes 12288 | tf_op jit(solution)/shard_map/gather | solution.py:417
  14.8 1.1 constant_dynamic-slice_fusion.refs_1_
  16.0 0.2 broadcast_multiply_fusion.right_ref
  16.2 56.4 %shard_map.86 = (bf16[3072,768]{1,0:T(8,128)(2,1)}, f32[1024,768]{1,0:T(8,128)S(1)}) custom-call(bf16[1024,3072]{1,0:T(8,128)(2,1)} %left_ref.3, bf16[384,768]{1,0:T(8,128)(2,1)S(1)} %constant_dynamic-slice_fusion.refs_1_), custom_call_target="tpu_custom_call" | custom-call | flops 4831838208 | bytes 37748736 | tf_op jit(solution)/shard_map/pallas_call | solution.py:115
  72.5 0.2 multiply_convert_fusion.right_ref
  72.8 48.6 %shard_map.87 = f32[384,768]{1,0:T(8,128)S(1)} custom-call(bf16[1024,3072]{1,0:T(8,128)(2,1)S(1)} %bitcast.3, bf16[1024,768]{1,0:T(8,128)(2,1)S(1)} %broadcast_multiply_fusion.right_ref), custom_call_target="tpu_custom_call" | custom-call | flops 4831838208 | bytes 37748736 | tf_op jit(solution)/shard_map/pallas_call | solution.py:197
  121.5 0.9 convert_element_type.24
  122.4 0.2 all-gather.5.cloned.1.call-start
  122.7 2.8 copy-done.3
  125.5 47.2 %shard_map.89 = f32[384,768]{1,0:T(8,128)S(1)} custom-call(bf16[1024,3072]{1,0:T(8,128)(2,1)S(1)} %copy-done.3, bf16[1024,768]{1,0:T(8,128)(2,1)S(1)} %multiply_convert_fusion.right_ref), custom_call_target="tpu_custom_call" | custom-call | flops 4831838208 | bytes 37748736 | tf_op jit(solution)/shard_map/pallas_call | solution.py:197
  172.7 2.0 add_convert_fusion
  174.8 5.2 %convolution_convert_fusion.refs_1_ = bf16[384,768]{1,0:T(8,128)(2,1)S(1)} fusion(bf16[384,3072]{1,0:T(8,128)(2,1)} %all-gather.3.cloned.1.call-done, bf16[3072,768]{1,0:T(8,128)(2,1)} %right_ref.1), kind=kOutput, calls=%fused_computation.2 | convolution fusion | flops 1812234240 | bytes 7667712 | tf_op jit(solution)/shard_map/dot_general | solution.py:17
  180.0 46.6 %shard_map.88 = (bf16[3072,768]{1,0:T(8,128)(2,1)S(1)}, f32[384,768]{1,0:T(8,128)S(1)}) custom-call(bf16[384,3072]{1,0:T(8,128)(2,1)S(1)} %copy-done.1, bf16[384,768]{1,0:T(8,128)(2,1)S(1)} %convolution_convert_fusion.refs_1_), custom_call_target="tpu_custom_call" | custom-call | flops 1811939328 | bytes 37748736 | tf_op jit(solution)/shard_map/pallas_call | solution.py:115
  226.6 2.1 copy-done.7
  228.8 2.3 copy-done.4
  231.1 1.7 copy-done.5
  232.8 2.3 copy-done.8
  235.1 18.4 %shard_map.90 = (f32[384,768]{1,0:T(8,128)S(1)}, bf16[384,768]{1,0:T(8,128)(2,1)S(1)}) custom-call(bf16[384,3072]{1,0:T(8,128)(2,1)S(1)} %copy-done.5, bf16[3072,768]{1,0:T(8,128)(2,1)S(1)} %copy-done.8, bf16[3072,768]{1,0:T(8,128)(2,1)S(1)} %copy-done.4), custom_call_target="tpu_custom_call" | custom-call | flops 3623878656 | bytes 9437184 | tf_op jit(solution)/shard_map/pallas_call | solution.py:275
  253.5 53.3 %shard_map.91 = (bf16[3072,768]{1,0:T(8,128)(2,1)}, f32[384,768]{1,0:T(8,128)S(1)}, f32[384,768]{1,0:T(8,128)S(1)}) custom-call(bf16[384,3072]{1,0:T(8,128)(2,1)S(1)} %copy-done.2, bf16[384,3072]{1,0:T(8,128)(2,1)S(1)} %copy-done.6, bf16[384,768]{1,0:T(8,128)(2,1)S(1)} %get-tuple-element.21.refs_2_), custom_call_target="tpu_custom_call" | custom-call | flops 3623878656 | bytes 37748736 | tf_op jit(solution)/shard_map/pallas_call | solution.py:115
  306.8 11.9 %shard_map.92 = (f32[384,768]{1,0:T(8,128)S(1)}, f32[384,768]{1,0:T(8,128)S(1)}) custom-call(f32[384,768]{1,0:T(8,128)S(1)} %neg.3.refs_0_, f32[384,768]{1,0:T(8,128)S(1)} %get-tuple-element.17.refs_1_, f32[384,768]{1,0:T(8,128)S(1)} %get-tuple-element.20.refs_2_, f32[384,768]{1,0:T(8,128)S(1)} %get-tuple-element.22.refs_3_, ...), custom_call_target="tpu_custom_call" | custom-call | tf_op jit(solution)/shard_map/pallas_call | solution.py:369
  318.7 1.0 copy.11
  319.7 1.0 copy.12
  (29 shorter events, 0.2 us)
Async XLA Ops:
  7.2 1.5 copy-start
  7.2 167.6 %all-gather.3.cloned.1.call-start = ((), (), s32[]{:S(2)}) async-start(), calls=%async_computation | async-start | bytes 2949120 | tf_op jit(solution)/shard_map/all_gather | solution.py:408
  8.6 6.2 %copy-start.10 = (s32[1024]{0:T(1024)S(1)}, s32[1024]{0:T(1024)}, u32[]{:S(2)}) copy-start(s32[1024]{0:T(1024)} %param.10) | copy-start | bytes 12292
  8.6 7.3 %copy-start.9 = (bf16[1024,768]{1,0:T(8,128)(2,1)S(1)}, bf16[1024,768]{1,0:T(8,128)(2,1)}, u32[]{:S(2)}) copy-start(bf16[1024,768]{1,0:T(8,128)(2,1)} %param.8) | copy-start | bytes 4718596
  15.9 56.9 %slice-start = ((s8[6291456]{0:T(1024)(128)(4,1)}), s8[4194304]{0:T(1024)(128)(4,1)S(1)}, s32[]{:S(2)}) async-start(s8[6291456]{0:T(1024)(128)(4,1)} %bitcast.2), calls=%async_computation.2 | async-start | bytes 8388608
  16.2 56.6 %slice-start.1 = ((s8[6291456]{0:T(1024)(128)(4,1)}), s8[2097152]{0:T(1024)(128)(4,1)S(1)}, s32[]{:S(2)}) async-start(s8[6291456]{0:T(1024)(128)(4,1)} %bitcast.2), calls=%async_computation.3 | async-start | bytes 4194304
  122.4 106.3 %all-gather.5.cloned.1.call-start = ((), (), s32[]{:S(2)}) async-start(), calls=%async_computation.1 | async-start | bytes 2949120 | tf_op jit(solution)/shard_map/all_gather | solution.py:408
  122.7 2.8 copy-start.3
  174.8 5.2 %copy-start.1 = (bf16[384,3072]{1,0:T(8,128)(2,1)S(1)}, bf16[384,3072]{1,0:T(8,128)(2,1)}, u32[]{:S(2)}) copy-start(bf16[384,3072]{1,0:T(8,128)(2,1)} %refs_0_.5) | copy-start | bytes 7077892
  226.6 2.1 copy-start.7
  228.8 2.3 copy-start.4
  231.1 1.7 copy-start.5
  232.8 2.3 copy-start.8
  235.1 18.4 %copy-start.2 = (bf16[384,3072]{1,0:T(8,128)(2,1)S(1)}, bf16[384,3072]{1,0:T(8,128)(2,1)}, u32[]{:S(2)}) copy-start(bf16[384,3072]{1,0:T(8,128)(2,1)} %refs_0_.5) | copy-start | bytes 7077892
  235.1 18.4 %copy-start.6 = (bf16[384,3072]{1,0:T(8,128)(2,1)S(1)}, bf16[384,3072]{1,0:T(8,128)(2,1)}, u32[]{:S(2)}) copy-start(bf16[384,3072]{1,0:T(8,128)(2,1)} %all-gather.5.cloned.1.call-done.both_ref.refs_1_) | copy-start | bytes 7077892
Sparse Core Ops, SparseCore 0:
  122.6 23.3 all-gather.2
  174.9 23.1 all-gather.4

commit v4 on v3

--- a/solution.py
+++ b/solution.py
@@ -10,7 +10,7 @@
 
 damping = 0.3
 MESH = pl.DeviceIdType.MESH
-VMEM_BYTES = 40 * 1024 * 1024
+VMEM_BYTES = 24 * 1024 * 1024
 
 
 def product(left, right):
@@ -42,16 +42,16 @@
     pl.semaphore_wait(barrier, len(neighbours))
 
 
-def gather_kernel(n, lefts, *refs):
-    left_refs, block_ref = refs[:lefts], refs[lefts]
-    full_ref, product_refs = refs[lefts + 1], refs[lefts + 2 : 2 * lefts + 2]
-    send_sem, recv_sem = refs[2 * lefts + 2 :]
-    rows, columns = block_ref.shape
+def gather_kernel(n, lefts, mixing, *refs):
+    left_refs, block_ref, refs = refs[:lefts], refs[lefts], refs[lefts + 1 :]
+    if mixing:
+        right_ref, refs = refs[0], refs[1:]
+    product_refs, full_ref = refs[:lefts], refs[lefts]
+    send_sem, recv_sem = refs[lefts + 1 :]
+    rows, columns = full_ref.shape[0] // n, full_ref.shape[1]
     half, piece = columns // 2, rows // 2
     me, place, following, preceding = ring(n)
     greet(({"fsdp": following}, {"fsdp": preceding}))
-
-    full_ref[pl.ds(pl.multiple_of(me * rows, rows), rows), :] = block_ref[...]
 
     def owner_at(step, way):
         return index_at((place + n - step) % n if way == 0 else (place + step) % n, n)
@@ -70,8 +70,14 @@
             device_id_type=MESH,
         )
 
-    for way in range(2):
-        for part in range(2):
+    for part in range(2):
+        for way in range(2):
+            lines, lanes = slice(part * piece, (part + 1) * piece), slice(way * half, (way + 1) * half)
+            if mixing:
+                block = product(block_ref[lines, :], right_ref[:, lanes]).astype(full_ref.dtype)
+            else:
+                block = block_ref[lines, lanes]
+            full_ref[pl.ds(pl.multiple_of(me * rows + part * piece, piece), piece), lanes] = block
             copy(0, way, part).start()
     for ref in product_refs:
         ref[...] = jnp.zeros_like(ref)
@@ -106,18 +112,23 @@
     lax.fori_loop(0, n - 1, settle, 0)
 
 
-def gather_products(lefts, block, number):
+def gather_products(lefts, block, number, right=None, keep=False):
     n = lax.axis_size("fsdp")
-    rows, columns = block.shape
+    rows, columns = block.shape[0], (block if right is None else right).shape[1]
+    operands = (*lefts, block) if right is None else (*lefts, block, right)
     vmem = pl.BlockSpec(memory_space=pltpu.VMEM)
-    outs = [jax.ShapeDtypeStruct((n * rows, columns), block.dtype)]
-    outs += [jax.ShapeDtypeStruct((left.shape[0], columns), jnp.float32) for left in lefts]
+    outs = [jax.ShapeDtypeStruct((left.shape[0], columns), jnp.float32) for left in lefts]
+    scratch = [pltpu.SemaphoreType.DMA((n - 1, 2, 2))] * 2
+    if keep:
+        outs.append(jax.ShapeDtypeStruct((n * rows, columns), block.dtype))
+    else:
+        scratch.insert(0, pltpu.VMEM((n * rows, columns), block.dtype))
     return pl.pallas_call(
-        functools.partial(gather_kernel, n, len(lefts)),
+        functools.partial(gather_kernel, n, len(lefts), right is not None),
         out_shape=outs,
-        in_specs=[vmem] * (len(lefts) + 1),
+        in_specs=[vmem] * len(operands),
         out_specs=[vmem] * len(outs),
-        scratch_shapes=[pltpu.SemaphoreType.DMA((n - 1, 2, 2))] * 2,
+        scratch_shapes=scratch,
         compiler_params=pltpu.CompilerParams(
             collective_id=number, has_side_effects=True, vmem_limit_bytes=VMEM_BYTES
         ),
@@ -126,7 +137,7 @@
             bytes_accessed=2 * n * rows * columns * 8,
             transcendentals=0,
         ),
-    )(*lefts, block)
+    )(*operands)
 
 
 def scatter_kernel(n, factor, left_ref, right_ref, out_ref, own, sent, held, send_sem, recv_sem):
@@ -383,6 +394,17 @@
     )(*blocks)
 
 
+def look_up(table, ids):
+    fold = 256
+    if table.shape[0] % fold:
+        return table[ids]
+    folded = table.reshape(-1, fold)
+    row, lane = ids[:, None] // fold, ids[:, None] % fold
+    chosen = (row == jnp.arange(folded.shape[0])).astype(jnp.float32)
+    near = jnp.dot(chosen, folded, precision=lax.Precision.HIGHEST)
+    return jnp.sum(jnp.where(lane == jnp.arange(fold), near, 0.0), axis=1)
+
+
 def body(activations, out_grads, token_ids, forget_mask, importance, in_inverse, out_inverse):
     low = jnp.bfloat16
     tok_rows = activations.shape[0]
@@ -409,12 +431,12 @@
 
     in_block = lax.dynamic_slice(in_inverse, (0, own), (in_inverse.shape[0], columns))
     if ringed:
-        _, tok_out = gather_products((activations,), in_block, 0)
+        (tok_out,) = gather_products((activations,), in_block, 0)
     else:
         tok_out = product(activations, all_rows(in_block))
 
     keep = 1.0 - forget_mask.astype(jnp.float32)
-    weights = importance[token_ids] * keep / total
+    weights = look_up(importance, token_ids) * keep / total
     forget_grads = out_grads * forget_mask.astype(low)[:, None]
     grad_scale = 1.0 / math.sqrt(total)
     scaled = (tok_out * weights[:, None]).astype(low)
@@ -428,11 +450,11 @@
     def mix(matrix):
         return product(all_columns(matrix.astype(low)), out_inverse).astype(low)
 
-    mixed = mix(start)
     if ringed:
-        mixed, precond_0 = gather_products((in_inverse,), mixed, 3)
+        wide = all_columns(start.astype(low))
+        precond_0, mixed = gather_products((in_inverse,), wide, 3, right=out_inverse, keep=True)
     else:
-        mixed = all_rows(mixed)
+        mixed = all_rows(mix(start))
         precond_0 = product(in_inverse, mixed)
     if ringed and lax.axis_size("fac") == 4:
         image_0, mixed = spread(both, mixed, out_inverse, 4)
@@ -440,7 +462,7 @@
         image_0 = product(both, mixed)
         mixed = mix(image_0)
     if ringed:
-        _, precond_1, image_1 = gather_products((in_inverse, both), mixed, 5)
+        precond_1, image_1 = gather_products((in_inverse, both), mixed, 5)
     else:
         mixed = all_rows(mixed)
         precond_1 = product(in_inverse, mixed)

time: 328 us -> 324 us (0.988)
  Pallas kernels: 282 us -> 276 us
  matrix products: 5.19 us -> 0.82 us
  other arithmetic: 4.81 us -> 8.33 us
  local copies, waits for them, and re-layouts: 20.6 us -> 24 us
    unnamed x28, local copies, waits for them, and re-layouts: 13.3 us -> 23 us
    pallas_call x3, Pallas kernels: 156 us -> 150 us  [gather_products(): pl.pallas_call(functools.partial(gather_kernel, n, len(lefts), right is n...]
    gather x1 -> x0, local copies, waits for them, and re-layouts: 6.15 us -> none  [body(): weights = importance[token_ids] * keep / total]
    dot_general x1, matrix products: 5.19 us -> 0.82 us  [look_up(): near = jnp.dot(chosen, folded, precision=lax.Precision.HIGHEST)]
  transfers between devices with their start and end apart: 2 -> 2, of which waited for: 0 -> 0; matrix products, arithmetic and copies ran while one was open for 2% -> 0% of each run, Pallas kernels for 29% -> 29%
where the time goes in v4:
time: 324 us; the launch traced here: 323 us
  Pallas kernels  276 us (85%)
  local copies, waits for them, and re-layouts  24 us (7%)
  between operations  14.2 us (4%)
  other arithmetic  8.33 us (3%)
    pallas_call x3, Pallas kernels, gather_products(): pl.pallas_call(functools.partial(gather_kernel, n, len(lefts), right is n...  150 us
    pallas_call x2, Pallas kernels, scatter_term(): pl.pallas_call(functools.partial(scatter_kernel, n, factor), out_shape=ja...  95.8 us
    unnamed x28, local copies, waits for them, and re-layouts  23 us
    pallas_call x1, Pallas kernels, spread(): pl.pallas_call(spread_kernel, out_shape=(jax.ShapeDtypeStruct((rows, colu...  18.2 us
    pallas_call x1, Pallas kernels, finish(): pl.pallas_call(functools.partial(finish_kernel, sizes), out_shape=(shape,...  12 us
  transfers between devices with their start and end apart: 2, of which 0 were waited for; matrix products, arithmetic and copies ran while one was open for 0% of the time, Pallas kernels for 29%

profile of v4, /device:TPU:0, one launch (start us, length us, event | category | flops | bytes accessed | tf_op | source)
XLA Modules:
  0.0 323.5 jit_solution(9405811087562385350)
XLA Ops:
  7.9 0.9 reshape.35
  11.1 2.9 broadcast_multiply_fusion.right_ref
  14.1 2.8 copy-done.8
  16.9 51.2 %shard_map.86 = f32[1024,768]{1,0:T(8,128)S(1)} custom-call(bf16[1024,3072]{1,0:T(8,128)(2,1)S(1)} %copy-done.8, bf16[384,768]{1,0:T(8,128)(2,1)S(1)} %constant_dynamic-slice_fusion.refs_1_), custom_call_target="tpu_custom_call" | custom-call | flops 4831838208 | bytes 37748736 | tf_op jit(solution)/shard_map/pallas_call | solution.py:126
  68.1 1.4 multiply_convert_fusion.right_ref
  70.0 48.6 %shard_map.87 = f32[384,768]{1,0:T(8,128)S(1)} custom-call(bf16[1024,3072]{1,0:T(8,128)(2,1)S(1)} %copy-done.8, bf16[1024,768]{1,0:T(8,128)(2,1)S(1)} %copy-done.5), custom_call_target="tpu_custom_call" | custom-call | flops 4831838208 | bytes 37748736 | tf_op jit(solution)/shard_map/pallas_call | solution.py:208
  118.7 0.9 convert_element_type.22
  119.9 1.4 copy-done.4
  121.3 2.8 copy-done.9
  124.1 47.2 %shard_map.89 = f32[384,768]{1,0:T(8,128)S(1)} custom-call(bf16[1024,3072]{1,0:T(8,128)(2,1)S(1)} %copy-done.9, bf16[1024,768]{1,0:T(8,128)(2,1)S(1)} %copy-done.4), custom_call_target="tpu_custom_call" | custom-call | flops 4831838208 | bytes 37748736 | tf_op jit(solution)/shard_map/pallas_call | solution.py:208
  171.3 1.0 add_convert_fusion
  172.3 2.3 copy-done.1
  174.7 1.7 copy-done.3
  176.3 47.1 %shard_map.88 = (f32[384,768]{1,0:T(8,128)S(1)}, bf16[3072,768]{1,0:T(8,128)(2,1)S(1)}) custom-call(bf16[384,3072]{1,0:T(8,128)(2,1)S(1)} %copy-done, bf16[384,3072]{1,0:T(8,128)(2,1)S(1)} %copy-done.3, bf16[3072,768]{1,0:T(8,128)(2,1)S(1)} %copy-done.1), custom_call_target="tpu_custom_call" | custom-call | flops 1811939328 | bytes 37748736 | tf_op jit(solution)/shard_map/pallas_call | solution.py:126
  223.5 1.0 copy-done.6
  224.5 2.1 copy-done.10
  226.6 2.3 copy-done.2
  229.0 2.3 copy-done.11
  231.3 1.7 copy-done.12
  233.0 18.2 %shard_map.90 = (f32[384,768]{1,0:T(8,128)S(1)}, bf16[384,768]{1,0:T(8,128)(2,1)S(1)}) custom-call(bf16[384,3072]{1,0:T(8,128)(2,1)S(1)} %copy-done.12, bf16[3072,768]{1,0:T(8,128)(2,1)S(1)} %copy-done.11, bf16[3072,768]{1,0:T(8,128)(2,1)S(1)} %copy-done.2), custom_call_target="tpu_custom_call" | custom-call | flops 3623878656 | bytes 9437184 | tf_op jit(solution)/shard_map/pallas_call | solution.py:286
  251.2 51.5 %shard_map.91 = (f32[384,768]{1,0:T(8,128)S(1)}, f32[384,768]{1,0:T(8,128)S(1)}) custom-call(bf16[384,3072]{1,0:T(8,128)(2,1)S(1)} %copy-done, bf16[384,3072]{1,0:T(8,128)(2,1)S(1)} %copy-done.12, bf16[384,768]{1,0:T(8,128)(2,1)S(1)} %get-tuple-element.19.refs_2_), custom_call_target="tpu_custom_call" | custom-call | flops 3623878656 | bytes 37748736 | tf_op jit(solution)/shard_map/pallas_call | solution.py:126
  302.6 12.0 %shard_map.92 = (f32[384,768]{1,0:T(8,128)S(1)}, f32[384,768]{1,0:T(8,128)S(1)}) custom-call(f32[384,768]{1,0:T(8,128)S(1)} %neg.3.refs_0_, f32[384,768]{1,0:T(8,128)S(1)} %copy-done.7, f32[384,768]{1,0:T(8,128)S(1)} %get-tuple-element.18.refs_2_, f32[384,768]{1,0:T(8,128)S(1)} %get-tuple-element.20.refs_3_, f32[384,768]{1,0:T(8,128)S(1)} %get-tuple-element.21.refs_4_), custom_call_target="tpu_custom_call" | custom-call | tf_op jit(solution)/shard_map/pallas_call | solution.py:380
  314.6 1.0 copy.11
  315.6 1.0 copy.12
  (28 shorter events, 3.9 us)
Async XLA Ops:
  7.2 165.2 %all-gather.3.cloned.1.call-start = ((), (), s32[]{:S(2)}) async-start(), calls=%async_computation | async-start | bytes 2949120 | tf_op jit(solution)/shard_map/all_gather | solution.py:430
  11.1 2.9 copy-start
  14.1 2.8 copy-start.8
  68.1 1.9 copy-start.5
  119.6 107.0 %all-gather.5.cloned.1.call-start = ((), (), s32[]{:S(2)}) async-start(), calls=%async_computation.1 | async-start | bytes 2949120 | tf_op jit(solution)/shard_map/all_gather | solution.py:430
  119.9 1.4 copy-start.4
  121.3 2.8 copy-start.9
  172.3 2.3 copy-start.1
  174.7 1.7 copy-start.3
  223.5 1.0 copy-start.6
  224.5 2.1 copy-start.10
  226.6 2.3 copy-start.2
  229.0 2.3 copy-start.11
  231.3 1.7 copy-start.12
  251.2 51.5 %copy-start.7 = (f32[384,768]{1,0:T(8,128)S(1)}, f32[384,768]{1,0:T(8,128)}, u32[]{:S(2)}) copy-start(f32[384,768]{1,0:T(8,128)} %copy-done.6) | copy-start | bytes 3538948
Sparse Core Ops, SparseCore 0:
  119.8 23.3 all-gather.2
  172.4 23.1 all-gather.4

commit v5 on v4

--- a/solution.py
+++ b/solution.py
@@ -10,7 +10,7 @@
 
 damping = 0.3
 MESH = pl.DeviceIdType.MESH
-VMEM_BYTES = 24 * 1024 * 1024
+VMEM_BYTES = 16 * 1024 * 1024
 
 
 def product(left, right):

time: 324 us -> 324 us (level)
    unnamed x28 -> x30, local copies, waits for them, and re-layouts: 23 us -> 23 us
where the time goes in v5:
time: 324 us
  Pallas kernels  276 us (85%)
  local copies, waits for them, and re-layouts  24 us (7%)
  between operations  14.2 us (4%)
  other arithmetic  8.34 us (3%)
    pallas_call x3, Pallas kernels, gather_products(): pl.pallas_call(functools.partial(gather_kernel, n, len(lefts), right is n...  150 us
    pallas_call x2, Pallas kernels, scatter_term(): pl.pallas_call(functools.partial(scatter_kernel, n, factor), out_shape=ja...  95.9 us
    unnamed x30, local copies, waits for them, and re-layouts  23 us
    pallas_call x1, Pallas kernels, spread(): pl.pallas_call(spread_kernel, out_shape=(jax.ShapeDtypeStruct((rows, colu...  18.1 us
    pallas_call x1, Pallas kernels, finish(): pl.pallas_call(functools.partial(finish_kernel, sizes), out_shape=(shape,...  12 us
  transfers between devices with their start and end apart: 2, of which 0 were waited for; matrix products, arithmetic and copies ran while one was open for 0% of the time, Pallas kernels for 29%

profile of v5, /device:TPU:0, one launch (start us, length us, event | category | flops | bytes accessed | tf_op | source)
XLA Modules:
  0.0 323.5 jit_solution(4388835405609795073)
XLA Ops:
  7.9 0.9 reshape.35
  11.1 2.9 broadcast_multiply_fusion.right_ref
  14.1 2.8 copy-done.8
  16.8 51.2 %shard_map.86 = f32[1024,768]{1,0:T(8,128)S(1)} custom-call(bf16[1024,3072]{1,0:T(8,128)(2,1)S(1)} %copy-done.8, bf16[384,768]{1,0:T(8,128)(2,1)S(1)} %constant_dynamic-slice_fusion.refs_1_), custom_call_target="tpu_custom_call" | custom-call | flops 4831838208 | bytes 37748736 | tf_op jit(solution)/shard_map/pallas_call | solution.py:126
  68.1 1.4 multiply_convert_fusion.right_ref
  70.0 48.7 %shard_map.87 = f32[384,768]{1,0:T(8,128)S(1)} custom-call(bf16[1024,3072]{1,0:T(8,128)(2,1)S(1)} %copy-done.9, bf16[1024,768]{1,0:T(8,128)(2,1)S(1)} %copy-done.5), custom_call_target="tpu_custom_call" | custom-call | flops 4831838208 | bytes 37748736 | tf_op jit(solution)/shard_map/pallas_call | solution.py:208
  118.8 0.9 convert_element_type.22
  119.9 1.4 copy-done.4
  121.3 2.8 copy-done.10
  124.1 47.2 %shard_map.89 = f32[384,768]{1,0:T(8,128)S(1)} custom-call(bf16[1024,3072]{1,0:T(8,128)(2,1)S(1)} %copy-done.10, bf16[1024,768]{1,0:T(8,128)(2,1)S(1)} %copy-done.4), custom_call_target="tpu_custom_call" | custom-call | flops 4831838208 | bytes 37748736 | tf_op jit(solution)/shard_map/pallas_call | solution.py:208
  171.3 1.0 add_convert_fusion
  172.4 2.3 copy-done.1
  174.7 1.7 copy-done.3
  176.4 47.1 %shard_map.88 = (f32[384,768]{1,0:T(8,128)S(1)}, bf16[3072,768]{1,0:T(8,128)(2,1)S(1)}) custom-call(bf16[384,3072]{1,0:T(8,128)(2,1)S(1)} %copy-done, bf16[384,3072]{1,0:T(8,128)(2,1)S(1)} %copy-done.3, bf16[3072,768]{1,0:T(8,128)(2,1)S(1)} %copy-done.1), custom_call_target="tpu_custom_call" | custom-call | flops 1811939328 | bytes 37748736 | tf_op jit(solution)/shard_map/pallas_call | solution.py:126
  223.5 1.0 copy-done.6
  224.5 2.1 copy-done.11
  226.7 2.3 copy-done.2
  229.0 2.3 copy-done.12
  231.3 1.7 copy-done.13
  233.0 18.1 %shard_map.90 = (f32[384,768]{1,0:T(8,128)S(1)}, bf16[384,768]{1,0:T(8,128)(2,1)S(1)}) custom-call(bf16[384,3072]{1,0:T(8,128)(2,1)S(1)} %copy-done.13, bf16[3072,768]{1,0:T(8,128)(2,1)S(1)} %copy-done.12, bf16[3072,768]{1,0:T(8,128)(2,1)S(1)} %copy-done.2), custom_call_target="tpu_custom_call" | custom-call | flops 3623878656 | bytes 9437184 | tf_op jit(solution)/shard_map/pallas_call | solution.py:286
  251.2 51.5 %shard_map.91 = (f32[384,768]{1,0:T(8,128)S(1)}, f32[384,768]{1,0:T(8,128)S(1)}) custom-call(bf16[384,3072]{1,0:T(8,128)(2,1)S(1)} %copy-done, bf16[384,3072]{1,0:T(8,128)(2,1)S(1)} %copy-done.13, bf16[384,768]{1,0:T(8,128)(2,1)S(1)} %get-tuple-element.19.refs_2_), custom_call_target="tpu_custom_call" | custom-call | flops 3623878656 | bytes 37748736 | tf_op jit(solution)/shard_map/pallas_call | solution.py:126
  302.6 12.0 %shard_map.92 = (f32[384,768]{1,0:T(8,128)S(1)}, f32[384,768]{1,0:T(8,128)S(1)}) custom-call(f32[384,768]{1,0:T(8,128)S(1)} %neg.3.refs_0_, f32[384,768]{1,0:T(8,128)S(1)} %copy-done.7, f32[384,768]{1,0:T(8,128)S(1)} %get-tuple-element.18.refs_2_, f32[384,768]{1,0:T(8,128)S(1)} %get-tuple-element.20.refs_3_, f32[384,768]{1,0:T(8,128)S(1)} %get-tuple-element.21.refs_4_), custom_call_target="tpu_custom_call" | custom-call | tf_op jit(solution)/shard_map/pallas_call | solution.py:380
  314.7 1.0 copy.11
  315.7 1.0 copy.12
  (30 shorter events, 3.9 us)
Async XLA Ops:
  7.2 165.2 %all-gather.3.cloned.1.call-start = ((), (), s32[]{:S(2)}) async-start(), calls=%async_computation | async-start | bytes 2949120 | tf_op jit(solution)/shard_map/all_gather | solution.py:430
  11.1 2.9 copy-start
  14.1 2.8 copy-start.8
  16.8 52.6 %copy-start.9 = (bf16[1024,3072]{1,0:T(8,128)(2,1)S(1)}, bf16[1024,3072]{1,0:T(8,128)(2,1)}, u32[]{:S(2)}) copy-start(bf16[1024,3072]{1,0:T(8,128)(2,1)} %left_ref.3) | copy-start | bytes 18874372
  68.1 1.9 copy-start.5
  119.7 107.0 %all-gather.5.cloned.1.call-start = ((), (), s32[]{:S(2)}) async-start(), calls=%async_computation.1 | async-start | bytes 2949120 | tf_op jit(solution)/shard_map/all_gather | solution.py:430
  119.9 1.4 copy-start.4
  121.3 2.8 copy-start.10
  172.4 2.3 copy-start.1
  174.7 1.7 copy-start.3
  223.5 1.0 copy-start.6
  224.5 2.1 copy-start.11
  226.7 2.3 copy-start.2
  229.0 2.3 copy-start.12
  231.3 1.7 copy-start.13
  251.1 51.5 %copy-start.7 = (f32[384,768]{1,0:T(8,128)S(1)}, f32[384,768]{1,0:T(8,128)}, u32[]{:S(2)}) copy-start(f32[384,768]{1,0:T(8,128)} %copy-done.6) | copy-start | bytes 3538948
Sparse Core Ops, SparseCore 0:
  119.8 23.3 all-gather.2
  172.4 23.1 all-gather.4
